TPU v7x, 128 devices: a whole 4x4x4 slice. The times are simulated.
128 devices in a mesh: fsdp: 32 (over y, x_hi, z), seq: 4 (over x_lo, core).
Axes of the slice: x: 4 (x_hi: 2, x_lo: 2; x = x_hi * 2 + x_lo), y: 4, z: 4, core: 2. Of those that a mesh axis runs over, the one named last changes fastest.
Arguments:
- inputs: bfloat16 [32768, 768], P(('fsdp', 'seq')), may hold values from -6 to 6
- proj_in: bfloat16 [768, 2304], P('fsdp'), may hold values from -0.21875 to 0.21875
- bias_query: bfloat16 [768], P('fsdp'), may hold values from -3 to 3
- bias_value: bfloat16 [768], P('fsdp'), may hold values from -3 to 3
- proj_out: bfloat16 [768, 768], P('fsdp'), may hold values from -0.625 to 0.625
- bias_out: bfloat16 [768], P('fsdp'), may hold values from -3 to 3
- norm_gain: bfloat16 [768], P('fsdp'), may hold values from 0.5 to 1.5
- norm_shift: bfloat16 [768], P('fsdp'), may hold values from -2 to 2
- up_weight: bfloat16 [768, 3072], P('fsdp'), may hold values from -0.21875 to 0.21875
- up_bias: bfloat16 [3072], P('fsdp'), may hold values from -3 to 3
- down_weight: bfloat16 [3072, 768], P('fsdp'), may hold values from -0.109375 to 0.109375
- down_bias: bfloat16 [768], P('fsdp'), may hold values from -3 to 3
- post_gain: bfloat16 [768], P('fsdp'), may hold values from 0.5 to 1.5
- post_shift: bfloat16 [768], P('fsdp'), may hold values from -2 to 2
- cotangent: bfloat16 [32768, 768], P(('fsdp', 'seq')), may hold values from -6 to 6
Outputs:
- output: bfloat16 [32768, 768], P(('fsdp', 'seq'))
- grad_input: bfloat16 [32768, 768], P(('fsdp', 'seq'))
- grad_proj_in: float32 [768, 2304], P('fsdp')
- grad_bias_query: float32 [768], P('fsdp')
- grad_bias_value: float32 [768], P('fsdp')
- grad_proj_out: float32 [768, 768], P('fsdp')
- grad_bias_out: float32 [768], P('fsdp')
- grad_norm_gain: float32 [768], P('fsdp')
- grad_norm_shift: float32 [768], P('fsdp')
- grad_up_weight: float32 [768, 3072], P('fsdp')
- grad_up_bias: float32 [3072], P('fsdp')
- grad_down_weight: float32 [3072, 768], P('fsdp')
- grad_down_bias: float32 [768], P('fsdp')
- grad_post_gain: float32 [768], P('fsdp')
- grad_post_shift: float32 [768], P('fsdp')
All inputs are finite; a program needn't handle non-finite values.
Results may differ from a plain program's by a relative error of at most 0.025.
Values may be sent and summed in bfloat16 or wider, within the bound.
A program may use at most 128 MiB of HBM per device.

v0:
```python
import functools
import math

import jax
import jax.numpy as jnp
from jax import lax
from jax.experimental import pallas as pl
from jax.experimental.pallas import tpu as pltpu
from jax.sharding import PartitionSpec as P

D = 768
H = 12
HD = 64
N = 32
G = 4
ROWS = 24
LEN = 1024
TOK = 256
HEADS = 3
OWN = HEADS * HD
PAD = 256
FFG = 768
epsilon = 1e-05
SCALE = 1.0 / math.sqrt(HD)
MESH = pl.DeviceIdType.MESH


def x_half(f):
    return lax.rem(f // 4, 2)


def place():
    return lax.axis_index("fsdp"), lax.axis_index("seq")


def fan_peer(f, s, t):
    peer = lax.rem(f + t, N)
    return peer, lax.rem(s + 2 * lax.abs(x_half(peer) - x_half(f)), G)


def row_server(f, s, i):
    owner = 8 * s + i
    away = lax.abs(x_half(owner) - x_half(f))
    lo = lax.rem(s // 2 + away, 2)
    return owner, 2 * lo + lax.rem(f, 2)


def row_client(f, s, m):
    group = f // 8
    away = lax.abs(s // 2 - group // 2)
    half = lax.rem(x_half(f) + away, 2)
    return (m // 2) * 8 + half * 4 + lax.rem(m, 2) * 2 + lax.rem(s, 2), group


def client_slot(f):
    return (f // 8) * 2 + lax.rem(f, 4) // 2


def send(src, dst, send_sem, recv_sem, f, s):
    pltpu.make_async_remote_copy(
        src_ref=src,
        dst_ref=dst,
        send_sem=send_sem,
        recv_sem=recv_sem,
        device_id=(f, s),
        device_id_type=MESH,
    ).start()


def take(ref, sem):
    pltpu.make_async_copy(ref, ref, sem).wait()


def loop(count, body):
    lax.fori_loop(0, count, lambda t, carry: (body(t), carry)[1], 0)


def greet(barrier, f, s):
    pl.semaphore_signal(barrier, inc=1, device_id=(f, s), device_id_type=MESH)


def greet_fan(barrier, f, s):
    loop(N - 1, lambda t: greet(barrier, *fan_peer(f, s, t + 1)))
    return N - 1


def greet_seq(barrier, f, s):
    loop(G - 1, lambda t: greet(barrier, f, lax.rem(s + t + 1, G)))
    return G - 1


def unless_self(f, s, peer, action):
    @pl.when(jnp.logical_or(peer[0] != f, peer[1] != s))
    def _():
        action(*peer)


def serves_self(f, s):
    return jnp.logical_and(f // 8 == s, row_server(f, s, lax.rem(f, 8))[1] == s)


def greet_rows(barrier, f, s, summed):
    peers = row_client if summed else row_server
    loop(8, lambda i: unless_self(f, s, peers(f, s, i), functools.partial(greet, barrier)))
    return 8 - serves_self(f, s).astype(jnp.int32)


def start_fan(kind, src, dst, sems, k, f, s):
    ss, rs, own = [group.at[k] for group in sems]
    block = {"fan": lambda pf, ps: src.at[ps], "fan_sum": lambda pf, ps: src.at[pf]}.get(kind, lambda pf, ps: src)

    def one(t):
        pf, ps = fan_peer(f, s, t + 1)
        send(block(pf, ps), dst.at[f], ss, rs, pf, ps)

    loop(N - 1, one)
    pltpu.make_async_copy(block(f, s), dst.at[f], own).start()


def start_seq(kind, src, dst, sems, k, f, s):
    ss, rs, own = [group.at[k] for group in sems]
    block = (lambda ps: src) if kind == "seq" else (lambda ps: src.at[ps])

    def one(t):
        ps = lax.rem(s + t + 1, G)
        send(block(ps), dst.at[s], ss, rs, f, ps)

    loop(G - 1, one)
    pltpu.make_async_copy(block(s), dst.at[s], own).start()


def start_rows(kind, src, dst, sems, k, f, s):
    ss, rs, own = [group.at[k] for group in sems]
    if kind == "rows":

        def one(m):
            unless_self(f, s, row_client(f, s, m), functools.partial(send, src, dst.at[lax.rem(f, 8)], ss, rs))
    else:

        def one(i):
            unless_self(
                f, s, row_server(f, s, i), functools.partial(send, src.at[i], dst.at[client_slot(f)], ss, rs)
            )

    loop(8, one)

    @pl.when(serves_self(f, s))
    def _():
        if kind == "rows":
            pltpu.make_async_copy(src, dst.at[lax.rem(f, 8)], own).start()
        else:
            pltpu.make_async_copy(src.at[lax.rem(f, 8)], dst.at[client_slot(f)], own).start()


def start(kind, *args):
    (start_fan if kind.startswith("fan") else start_seq if kind.startswith("seq") else start_rows)(kind, *args)


def finish(kind, dst, sems, k, f, s, part):
    ss, rs, own = [group.at[k] for group in sems]
    remote = rs if part == "recv" else ss
    if kind.startswith("rows"):

        @pl.when(serves_self(f, s))
        def _():
            if part == "recv":
                take(dst.at[0], own)
            take(dst.at[pl.ds(0, 7)], remote)

        @pl.when(jnp.logical_not(serves_self(f, s)))
        def _():
            take(dst, remote)
    else:
        if part == "recv":
            take(dst.at[0], own)
        take(dst.at[pl.ds(0, dst.shape[0] - 1)], remote)


def exchange_kernel(kinds, *refs):
    n = len(kinds)
    srcs, dsts, sems = refs[:n], refs[n : 2 * n], refs[2 * n :]
    f, s = place()
    barrier = pltpu.get_barrier_semaphore()
    expected = 0
    if any(k.startswith("fan") for k in kinds):
        expected += greet_fan(barrier, f, s)
    if any(k.startswith("seq") for k in kinds):
        expected += greet_seq(barrier, f, s)
    if "rows" in kinds:
        expected += greet_rows(barrier, f, s, False)
    if "rows_sum" in kinds:
        expected += greet_rows(barrier, f, s, True)
    pl.semaphore_wait(barrier, expected)
    for k, kind in enumerate(kinds):
        start(kind, srcs[k], dsts[k], sems, k, f, s)
    for k, kind in enumerate(kinds):
        finish(kind, dsts[k], sems, k, f, s, "recv")
        finish(kind, dsts[k], sems, k, f, s, "send")


def exchange(collective_id, kinds, arrays):
    shapes = []
    for kind, array in zip(kinds, arrays):
        block = array.shape if kind in ("fan_whole", "seq", "rows") else array.shape[1:]
        count = N if kind.startswith("fan") else G if kind.startswith("seq") else 8
        shapes.append(jax.ShapeDtypeStruct((count,) + block, array.dtype))
    n = len(kinds)
    return pl.pallas_call(
        functools.partial(exchange_kernel, kinds),
        out_shape=shapes,
        in_specs=[pl.BlockSpec(memory_space=pl.ANY)] * n,
        out_specs=[pl.BlockSpec(memory_space=pl.ANY)] * n,
        scratch_shapes=[pltpu.SemaphoreType.DMA((n,))] * 3,
        compiler_params=pltpu.CompilerParams(collective_id=collective_id, has_side_effects=True),
    )(*arrays)


def pack(blocks):
    c = blocks.shape[-1] // 2
    return jnp.concatenate([blocks[..., :c], blocks[..., c:]], axis=-2)


def unpack(blocks):
    return jnp.concatenate([blocks[..., :ROWS, :], blocks[..., ROWS:, :]], axis=-1)


def pad_heads(blocks):
    return jnp.pad(blocks, [(0, 0)] * (blocks.ndim - 1) + [(0, PAD - OWN)])


def norm_parts(values):
    center = jnp.mean(values, axis=-1, keepdims=True)
    centered = values - center
    spread = jnp.mean(centered * centered, axis=-1, keepdims=True)
    inverse = lax.rsqrt(spread + epsilon)
    return centered * inverse, inverse


def norm_back(grad, gain, unit, inverse):
    scaled = grad * gain
    mean_one = jnp.mean(scaled, axis=-1, keepdims=True)
    mean_two = jnp.mean(scaled * unit, axis=-1, keepdims=True)
    return inverse * (scaled - mean_one - unit * mean_two)


def dot(a, b):
    return jnp.dot(a, b, preferred_element_type=jnp.float32)


def dot_t(a, b):
    return lax.dot_general(a, b, (((1,), (1,)), ((), ())), preferred_element_type=jnp.float32)


def t_dot(a, b):
    return lax.dot_general(a, b, (((0,), (0,)), ((), ())), preferred_element_type=jnp.float32)


def tile(t, size=TOK):
    return pl.ds(pl.multiple_of(t * size, size), size)


def unpack_into(packed, wide):
    c = packed.shape[-1]

    def pair(p):
        one = packed[2 * p].astype(jnp.float32)
        two = packed[2 * p + 1].astype(jnp.float32)
        rows = pl.ds(pl.multiple_of(48 * p, 48), 48)
        wide[rows, :c] = jnp.concatenate([one[:ROWS], two[:ROWS]], axis=0).astype(wide.dtype)
        wide[rows, c:] = jnp.concatenate([one[ROWS:], two[ROWS:]], axis=0).astype(wide.dtype)

    loop(N // 2, pair)


def lanes_of(h, shape):
    lane = lax.broadcasted_iota(jnp.int32, shape, 1)
    return lane < HD if h % 2 == 0 else lane >= HD


def only(h, block):
    return jnp.where(lanes_of(h, block.shape), block, jnp.zeros_like(block))


def causal(scores, offset):
    row = offset + lax.broadcasted_iota(jnp.int32, scores.shape, 0)
    col = lax.broadcasted_iota(jnp.int32, scores.shape, 1)
    return jnp.where(col <= row, scores, -1e9)


class Ring:
    def __init__(self, src, held, sends, recvs, own, order, f, s):
        self.src, self.held, self.sends, self.recvs, self.own = src, held, sends, recvs, own
        self.order, self.f, self.s = order, f, s
        self.y, self.h, self.z = f // 8, x_half(f), lax.rem(f, 4)

    def peer(self, axis, step):
        if axis == "y":
            return lax.rem(self.y + step + 4, 4) * 8 + lax.rem(self.f, 8), self.s
        return self.f - self.z + lax.rem(self.z + step + 4, 4), self.s

    def coordinate(self, axis, step):
        return lax.rem((self.y if axis == "y" else self.z) + step + 4, 4)

    def one(self, axis, step, half=None):
        i = self.coordinate(axis, step)
        halves = slice(None) if half is None else half
        return self.held.at[i, halves, self.z] if axis == "y" else self.held.at[self.y, halves, i]

    def many(self, axis, step, half=None):
        i = self.coordinate(axis, step)
        if axis == "y":
            return self.held.at[i] if half is None else self.held.at[i, half]
        rows = slice(None) if half is None else slice(2 * half, 2 * half + 2)
        return self.held.at[rows, slice(None), i]

    def push(self, block, k, peer):
        send(block, block, self.sends.at[k], self.recvs.at[k], *peer)

    def begin(self):
        mine = self.held.at[self.y, self.h, self.z]
        other = lax.rem(self.s + 2, G)
        send(
            self.src.at[other], mine, self.sends.at[0], self.recvs.at[0], self.f + 4 - 8 * self.h, other
        )
        pltpu.make_async_copy(self.src.at[self.s], mine, self.own.at[0]).start()

    def first(self):
        mine = self.held.at[self.y, self.h, self.z]
        take(mine, self.own.at[0])
        take(mine, self.recvs.at[0])
        axis = self.order[0]
        self.push(self.one(axis, 0), 1, self.peer(axis, 1))
        self.push(self.one(axis, 0), 2, self.peer(axis, -1))

    def relay(self, part, base, axis):
        take(part(axis, -1), self.recvs.at[base])
        self.push(part(axis, -1, 0), base + 2, self.peer(axis, 1))
        take(part(axis, 1), self.recvs.at[base + 1])
        self.push(part(axis, 1, 1), base + 3, self.peer(axis, -1))

    def first_relay(self):
        self.relay(self.one, 1, self.order[0])

    def last(self):
        axis = self.order[0]
        take(self.one(axis, 2, 0), self.recvs.at[3])
        take(self.one(axis, 2, 1), self.recvs.at[4])
        axis = self.order[1]
        self.push(self.many(axis, 0), 5, self.peer(axis, 1))
        self.push(self.many(axis, 0), 6, self.peer(axis, -1))

    def last_relay(self):
        self.relay(self.many, 5, self.order[1])

    def arrive(self):
        axis = self.order[1]
        take(self.many(axis, 2, 0), self.recvs.at[7])
        take(self.many(axis, 2, 1), self.recvs.at[8])

    def drain(self):
        one, many = self.order
        take(self.held.at[self.y, self.h, self.z], self.sends.at[0])
        for k in (1, 2):
            take(self.one(one, 0), self.sends.at[k])
            take(self.one(one, 0, 0), self.sends.at[k + 2])
            take(self.many(many, 0), self.sends.at[k + 4])
            take(self.many(many, 0, 0), self.sends.at[k + 6])


class Share:
    def __init__(self, block, sends, recvs, f, s):
        self.block, self.sends, self.recvs, self.f, self.s = block, sends, recvs, f, s
        self.twin = s + 1 - 2 * lax.rem(s, 2)
        self.across = lax.rem(s + 2, G)

    def begin(self):
        mine = self.block(self.s)
        send(mine, mine, self.sends.at[1], self.recvs.at[1], self.f, self.across)
        send(mine, mine, self.sends.at[0], self.recvs.at[0], self.f, self.twin)

    def relay(self):
        theirs = self.block(self.across)
        take(theirs, self.recvs.at[1])
        send(theirs, theirs, self.sends.at[2], self.recvs.at[2], self.f, self.twin)

    def arrive(self):
        take(self.block(self.s), self.recvs.at[0])
        take(self.block(self.s), self.recvs.at[2])

    def drain(self):
        for k in range(3):
            take(self.block(self.s), self.sends.at[k])


def greet_near(barrier, f, s):
    y, h, z = f // 8, x_half(f), lax.rem(f, 4)
    greet(barrier, f + 4 - 8 * h, lax.rem(s + 2, G))
    for step in (1, 3):
        greet(barrier, lax.rem(y + step, 4) * 8 + lax.rem(f, 8), s)
        greet(barrier, f - z + lax.rem(z + step, 4), s)
    for step in (1, 2, 3):
        greet(barrier, f, lax.rem(s + step, G))
    pl.semaphore_wait(barrier, 8)


def unpack_rings(held, first, wide):
    c = held.shape[-1]

    def pair(p):
        at = (p // 4, lax.rem(p // 2, 2))
        z = 2 * lax.rem(p, 2)
        one = held[at[0], at[1], z, first : first + 48, :].astype(jnp.float32)
        two = held[at[0], at[1], z + 1, first : first + 48, :].astype(jnp.float32)
        rows = pl.ds(pl.multiple_of(48 * p, 48), 48)
        wide[rows, :c] = jnp.concatenate([one[:ROWS], two[:ROWS]], axis=0).astype(wide.dtype)
        wide[rows, c:] = jnp.concatenate([one[ROWS:], two[ROWS:]], axis=0).astype(wide.dtype)

    loop(N // 2, pair)


def spread_vectors(held, vec, f, s):
    low, full = jnp.bfloat16, jnp.float32
    row = lax.broadcasted_iota(jnp.int32, (128, D), 0)
    lane = lax.broadcasted_iota(jnp.int32, (128, D), 1)
    inside = lax.rem(lane, ROWS)
    plain = (row == inside).astype(full).astype(low)
    shifted = (row == inside + ROWS * s).astype(full).astype(low)
    owner = lax.broadcasted_iota(jnp.int32, (16, D), 1) // ROWS
    number = lax.broadcasted_iota(jnp.int32, (16, D), 0)
    vec[...] = jnp.zeros_like(vec)

    def add(j):
        block = held[j // 8, lax.rem(j // 4, 2), lax.rem(j, 4), 48:64, :128]
        straight, moved = dot(block, plain), dot(block, shifted)
        wanted = jnp.where(number < 7, j, jnp.where(j // 8 == s, lax.rem(j, 8), -1))
        vec[...] += jnp.where(owner == wanted, jnp.where(number == 6, moved, straight), 0.0)

    loop(N, add)


def forward_kernel(
    src_a, src_b, src_c, src_x, src_dy,
    got_x, vec, normed, qkv, w_in, lse, got_ctx, w_out, w_up, w_down, got_dy,
    held_a, held_b, held_c, ring_ss, ring_rs, ring_own, seq_ss, seq_rs, seq_own,
):
    f, s = place()
    greet_near(pltpu.get_barrier_semaphore(), f, s)
    ring_a, ring_b, ring_c = [
        Ring(src, held, ring_ss.at[k], ring_rs.at[k], ring_own.at[k], order, f, s)
        for k, (src, held, order) in enumerate(
            ((src_a, held_a, "yz"), (src_b, held_b, "zy"), (src_c, held_c, "yz"))
        )
    ]
    rings = (ring_a, ring_b, ring_c)
    copies = [
        pltpu.make_async_copy(src, dst.at[s], seq_own.at[k])
        for k, (src, dst) in enumerate(((src_x, got_x), (src_dy, got_dy)))
    ]
    for copy in copies:
        copy.start()
    for ring in rings:
        ring.begin()
    share_x, share_dy = [
        Share(lambda i, dst=dst: dst.at[i], seq_ss.at[k], seq_rs.at[k], f, s)
        for k, dst in enumerate((got_x, got_dy))
    ]
    copies[0].wait()
    share_x.begin()
    for ring in rings:
        ring.first()
    for ring in rings:
        ring.first_relay()
    for ring in rings:
        ring.last()
    share_x.relay()
    copies[1].wait()
    share_dy.begin()
    share_x.arrive()
    for ring in rings:
        ring.last_relay()
    ring_a.arrive()
    spread_vectors(held_a, vec, f, s)
    gain, shift = vec[0:1, :], vec[1:2, :]

    def norm_tile(t):
        unit, _ = norm_parts(got_x[t].astype(jnp.float32))
        normed[tile(t), :] = (unit * gain + shift).astype(normed.dtype)

    loop(G, norm_tile)
    unpack_rings(held_a, 0, w_in)
    bias = jnp.concatenate([vec[7:8, :PAD], jnp.zeros((1, PAD), jnp.float32), vec[8:9, :PAD]], axis=1)

    def project(t):
        made = (dot(normed[tile(t), :], w_in[...]) + bias).astype(qkv.dtype)
        qkv[tile(t), :PAD] = (made[:, :PAD].astype(jnp.float32) * SCALE).astype(qkv.dtype)
        qkv[tile(t), PAD:] = made[:, PAD:]

    loop(G, project)
    share_dy.relay()
    shares = []
    for step, b in enumerate((3, 2, 1, 0)):
        rows, span = slice(b * TOK, (b + 1) * TOK), (b + 1) * TOK
        for pair in range(2):
            at = pair * 128
            made = None
            for h in range(2 * pair, min(2 * pair + 2, HEADS)):
                query = only(h, qkv[rows, at : at + 128])
                scores = causal(dot_t(query, qkv[:span, PAD + at : PAD + at + 128]), b * TOK)
                peak = jnp.max(scores, axis=-1, keepdims=True)
                weights = jnp.exp(scores - peak)
                total = jnp.sum(weights, axis=-1, keepdims=True)
                lse[h, rows, :] = peak + jnp.log(total)
                part = dot(weights.astype(qkv.dtype), qkv[:span, 2 * PAD + at : 2 * PAD + at + 128]) / total
                made = part if made is None else jnp.where(lanes_of(h, part.shape), part, made)
            got_ctx[s, rows, at : at + 128] = made.astype(got_ctx.dtype)
        shares.append(
            Share(
                lambda i, b=b: got_ctx.at[i, pl.ds(b * TOK, TOK)], seq_ss.at[2 + step], seq_rs.at[2 + step], f, s
            )
        )
        shares[-1].begin()
        if step:
            shares[step - 1].relay()
    shares[-1].relay()
    ring_b.arrive()
    unpack_rings(held_b, 0, w_out)
    unpack_rings(held_b, 48, w_up)
    ring_c.arrive()
    unpack_rings(held_c, 0, w_down)
    share_dy.arrive()
    for share in shares:
        share.arrive()
    for share in [share_x, share_dy] + shares:
        share.drain()
    for ring in rings:
        ring.drain()


def forward(src_a, src_b, src_c, inputs, cotangent):
    low, full = jnp.bfloat16, jnp.float32
    any_space, vmem = pl.BlockSpec(memory_space=pl.ANY), pl.BlockSpec(memory_space=pltpu.VMEM)
    shape = jax.ShapeDtypeStruct
    outs = (
        shape((G, TOK, D), low),
        shape((16, D), full),
        shape((LEN, D), low),
        shape((LEN, 3 * PAD), low),
        shape((D, 3 * PAD), low),
        shape((HEADS, LEN, 1), full),
        shape((G, LEN, PAD), low),
        shape((D, D), low),
        shape((D, FFG), low),
        shape((FFG, D), low),
        shape((G, TOK, D), low),
    )
    return pl.pallas_call(
        forward_kernel,
        out_shape=outs,
        in_specs=[any_space] * 5,
        out_specs=[vmem] * len(outs),
        scratch_shapes=[pltpu.VMEM((4, 2, 4, rows, 384), low) for rows in (64, 96, 48)]
        + [pltpu.SemaphoreType.DMA((3, 9))] * 2
        + [pltpu.SemaphoreType.DMA((3, 1))]
        + [pltpu.SemaphoreType.DMA((6, 3))] * 2
        + [pltpu.SemaphoreType.DMA((2,))],
        compiler_params=pltpu.CompilerParams(
            collective_id=0, has_side_effects=True, vmem_limit_bytes=48 * 2**20
        ),
    )(src_a, src_b, src_c, inputs, cotangent)


def on_device(
    inputs,
    proj_in,
    bias_query,
    bias_value,
    proj_out,
    bias_out,
    norm_gain,
    norm_shift,
    up_weight,
    up_bias,
    down_weight,
    down_bias,
    post_gain,
    post_shift,
    cotangent,
):
    low = jnp.bfloat16
    full = jnp.float32
    f, s = place()
    split = proj_in.reshape(ROWS, 3, G, OWN).transpose(2, 0, 1, 3)
    send_in = pack(pad_heads(split).reshape(G, ROWS, 3 * PAD))
    units = up_weight.reshape(ROWS, N, G, ROWS).transpose(2, 0, 1, 3).reshape(G, ROWS, FFG)
    send_out = jnp.broadcast_to(pack(proj_out)[None], (G, 48, 384))
    vectors = jnp.stack(
        [norm_gain, norm_shift, post_gain, post_shift, bias_out, down_bias, jnp.zeros_like(bias_out), bias_query, bias_value]
    )
    compact = jnp.pad(vectors, ((0, 7), (0, 384 - ROWS)))
    compact = compact + jnp.pad(up_bias[None], ((6, 9), (0, 384 - 96)))
    src_a = jnp.concatenate([send_in, jnp.broadcast_to(compact[None], (G, 16, 384))], axis=1)
    src_b = jnp.concatenate([send_out, pack(units)], axis=1)
    src_c = pack(down_weight.reshape(G, ROWS, D))
    got_x, vec, normed, qkv, w_in, lse, got_ctx, w_out, w_up, w_down, got_dy = forward(
        src_a, src_b, src_c, inputs, cotangent
    )
    gain_one, shift_one, gain_two, shift_two, out_shift, down_shift = [vec[i] for i in range(6)]
    up_shift = vec[6]

    x = got_x.reshape(LEN, D).astype(full)
    dy = got_dy.reshape(LEN, D)
    unit_one, inverse_one = norm_parts(x)
    heads = qkv.reshape(LEN, 3, PAD)[:, :, :OWN].reshape(LEN, 3, HEADS, HD).transpose(1, 2, 0, 3)
    queries, keys, values = heads[0], heads[1], heads[2]
    scores = jnp.einsum("hqd,hkd->hqk", queries, keys, preferred_element_type=full)
    mask = jnp.arange(LEN)[None, :] <= jnp.arange(LEN)[:, None]
    probs = jnp.exp(jnp.where(mask, scores, -1e9) - lse)
    probs_low = probs.astype(low)
    context = got_ctx[:, :, :OWN].transpose(1, 0, 2).reshape(LEN, D)

    residual = x + dot(context, w_out) + out_shift
    unit_two, inverse_two = norm_parts(residual)
    normed_two = (unit_two * gain_two + shift_two).astype(low)
    hidden = dot(normed_two, w_up) + up_shift
    active, pull_gelu = jax.vjp(functools.partial(jax.nn.gelu, approximate=False), hidden)
    active_low = active.astype(low)
    out_part = dot(active_low, w_down).astype(low).reshape(G, TOK, D)
    grad_down = t_dot(active_low, dy)
    d_hidden = pull_gelu(dot_t(dy, w_down))[0].astype(low)
    grad_up = t_dot(normed_two, d_hidden)
    grad_up_bias = jnp.sum(d_hidden.astype(full), axis=0)
    d_two_part = dot_t(d_hidden, w_up).astype(low).reshape(G, TOK, D)
    got_two, got_outs = exchange(2, ("seq_sum", "seq_sum"), (d_two_part, out_part))

    def own(array):
        return lax.dynamic_slice_in_dim(array, s * TOK, TOK)

    output = (own(residual) + jnp.sum(got_outs.astype(full), axis=0) + down_shift).astype(low)
    d_two = jnp.sum(got_two.astype(full), axis=0)
    unit_own, cot = own(unit_two), cotangent.astype(full)
    grad_post_gain = jnp.sum(d_two * unit_own, axis=0)
    grad_post_shift = jnp.sum(d_two, axis=0)
    d_residual = cot + norm_back(d_two, gain_two, unit_own, own(inverse_two))
    branch_own = d_residual.astype(low)
    (got_branch,) = exchange(3, ("seq",), (branch_own,))
    branch = got_branch.reshape(LEN, D)
    w_out_own = lax.dynamic_slice_in_dim(w_out, s * OWN, OWN)
    d_ctx = dot_t(branch, w_out_own).astype(low)
    grad_out = t_dot(context, pad_heads(lax.dynamic_slice_in_dim(branch, s * OWN, OWN, 1)))
    d_ctx_heads = d_ctx.reshape(LEN, HEADS, HD).transpose(1, 0, 2)
    d_values = jnp.einsum("hqk,hqd->hkd", probs_low, d_ctx_heads, preferred_element_type=full)
    d_probs = jnp.einsum("hqd,hkd->hqk", d_ctx_heads, values, preferred_element_type=full)
    inner = jnp.sum(probs * d_probs, axis=-1, keepdims=True)
    d_scores = (probs * (d_probs - inner)).astype(low)
    d_queries = jnp.einsum("hqk,hkd->hqd", d_scores, keys, preferred_element_type=full) * SCALE
    d_keys = jnp.einsum("hqk,hqd->hkd", d_scores, queries, preferred_element_type=full)
    d_proj = jnp.stack([d_queries, d_keys, d_values]).transpose(2, 0, 1, 3).reshape(LEN, 3, OWN)
    d_proj = pad_heads(d_proj).astype(low).reshape(LEN, 3 * PAD)
    grad_in = t_dot(normed, d_proj)
    d_bias = jnp.sum(d_proj.astype(full), axis=0)
    d_one_part = dot_t(d_proj, w_in).astype(low).reshape(G, TOK, D)
    (got_one,) = exchange(4, ("seq_sum",), (d_one_part,))
    d_one = jnp.sum(got_one.astype(full), axis=0)
    unit_first = own(unit_one)
    grad_input = d_residual + norm_back(d_one, gain_one, unit_first, own(inverse_one))
    zero = jnp.zeros((D,), full)
    sums = jnp.stack(
        [
            jnp.sum(d_one * unit_first, axis=0),
            jnp.sum(d_one, axis=0),
            grad_post_gain,
            grad_post_shift,
            jnp.sum(branch_own.astype(full), axis=0),
            jnp.sum(cot, axis=0),
            lax.dynamic_update_slice_in_dim(zero, d_bias[:OWN], s * OWN, 0),
            lax.dynamic_update_slice_in_dim(zero, d_bias[2 * PAD : 2 * PAD + OWN], s * OWN, 0),
        ]
    )
    sums_up = lax.dynamic_update_slice_in_dim(jnp.zeros((4, D), full), grad_up_bias[None], s, 0)
    sums = jnp.pad(jnp.concatenate([sums, sums_up]), ((0, 116), (0, 0)))
    vec_blocks = sums.T.reshape(N, ROWS, 128)

    def cut(grad):
        return pack(grad.reshape(N, ROWS, -1)).astype(low)

    part_in, part_up, part_out, part_down, part_vec = exchange(
        5,
        ("fan_sum",) * 5,
        (cut(grad_in), cut(grad_up), cut(grad_out), cut(grad_down), vec_blocks),
    )

    def halves(part):
        wide = part.astype(full).reshape(4, 2, 4, *part.shape[1:])
        wide = jnp.sum(wide, axis=(0, 2))
        mine = lax.dynamic_index_in_dim(wide, x_half(f), keepdims=False)
        other = lax.dynamic_index_in_dim(wide, 1 - x_half(f), keepdims=False)
        return jnp.stack([mine, other])

    share = (
        halves(part_in).astype(low),
        halves(part_up).astype(low),
        halves(part_out).astype(low),
        halves(part_down).astype(low),
        jnp.sum(part_vec, axis=0),
    )
    all_in, all_up_g, all_out, all_down, all_vec = exchange(6, ("seq",) * 5, share)

    def groups(parts):
        wide = parts.astype(full)
        swapped = jnp.concatenate([wide[2:, 1], wide[:2, 1]])
        return unpack(wide[:, 0] + swapped)

    final_in = groups(all_in).reshape(G, ROWS, 3, PAD)[..., :OWN].transpose(1, 2, 0, 3)
    final_up = groups(all_up_g).reshape(G, ROWS, N, ROWS).transpose(1, 2, 0, 3).reshape(ROWS, G * FFG)
    final_out = groups(all_out)[..., :OWN].transpose(1, 0, 2).reshape(ROWS, D)
    final_down = groups(all_down).reshape(96, D)
    final_vec = jnp.sum(all_vec, axis=0).T
    return (
        output,
        grad_input.astype(low),
        final_in.reshape(ROWS, 3 * D),
        final_vec[6],
        final_vec[7],
        final_out,
        final_vec[4],
        final_vec[0],
        final_vec[1],
        final_up,
        final_vec[8:12].reshape(96),
        final_down,
        final_vec[5],
        final_vec[2],
        final_vec[3],
    )


def solution(mesh):
    rows, wide, flat = P(("fsdp", "seq"), None), P("fsdp", None), P("fsdp")
    return jax.shard_map(
        on_device,
        mesh=mesh,
        in_specs=(rows, wide, flat, flat, wide, flat, flat, flat, wide, flat, wide, flat, flat, flat, rows),
        out_specs=(rows, rows, wide, flat, flat, wide, flat, flat, flat, wide, flat, wide, flat, flat, flat),
        check_vma=False,
    )
```

profile of v0, /device:TPU:1, one launch (start us, length us, event | category | flops | bytes accessed | tf_op | source)
XLA Modules:
  0.0 376.6 jit_solution(14123790844824768896)
XLA Ops:
  0.7 1.5 stack.99
  6.2 1.2 reshape.239
  7.6 1.2 reshape.240
  8.8 1.3 iota_compare_fusion
  10.2 70.7 %shard_map.262 = (bf16[4,256,768]{2,1,0:T(8,128)(2,1)}, f32[16,768]{1,0:T(8,128)S(1)}, bf16[1024,768]{1,0:T(8,128)(2,1)}, bf16[1024,768]{1,0:T(8,128)(2,1)}, bf1...) custom-call(bf16[4,64,384]{2,1,0:T(8,128)(2,1)S(1)} %pad_maximum_fus, ...), custom_call_target="tpu_custom_call" | custom-call | tf_op jit(solution)/shard_map/pallas_call | solution.py:556
  83.0 3.0 slice_bitcast_fusion
  86.0 3.9 %copy.141 = bf16[1024,4,192]{0,2,1:T(8,128)(2,1)} copy(bf16[1024,4,192]{2,0,1:T(8,128)(2,1)} %slice_bitcast_fusion) | data formatting | bytes 3145728 | tf_op jit(solution)/shard_map/transpose | solution.py:619
  89.9 1.7 convert_reduce_fusion.10
  91.7 2.0 multiply_reduce_fusion.1
  93.8 1.9 reduce.10
  95.8 3.4 bitcast_convert_fusion
  99.2 2.6 copy.145
  101.8 2.4 slice.254
  104.2 3.0 copy.149
  107.2 4.4 %fusion.71 = (f32[1024]{0:T(1024)S(1)}, f32[1024,768]{1,0:T(8,128)S(1)}) fusion(f32[768]{0:T(1024)S(1)} %get-tuple-element.76, f32[1024,768]{1,0:T(8,128)} %bitcast_convert_fusion, bf16[1024,768]{0,1:T(8,128)(2,1)} %bitcast.244, bf16[768,768]{1,0:T(8,128)(2,1)} %copy-done.2), kind=kOutput, calls=%fused_computation.194 | convolution fusion | flops 1210317824 | bytes 9051136 | tf_op jit(solution)/shard_map/dot_general | solution.py:247
  114.0 8.1 %fusion.7 = (bf16[768,1024]{1,0:T(8,128)(2,1)S(1)}, f32[1024,768]{0,1:T(8,128)S(1)}) fusion(f32[768]{0:T(1024)S(1)} %get-tuple-element.73, bf16[768,768]{1,0:T(8,128)(2,1)S(1)} %copy-done.4, f32[1024,768]{1,0:T(8,128)S(1)} %subtract_multiply_fusion, f32[768]{0:T(1024)S(1)} %get-tuple-element.74, f32[768]{0:T(1024)S(1)} %get-tuple-element.75), kind=kOutput, calls=%fused_computation.16 | convolution fusion | flops 1262223360 | bytes 9053184 | tf_op jit(solution)/shard_map/dot_general | solution.py:247
  122.0 1.4 convolution_convert_fusion.3
  124.6 11.0 %convert_reduce_fusion.4 = (f32[768]{0:T(1024)S(1)}, bf16[1024,768]{0,1:T(8,128)(2,1)}, f32[1024,768]{0,1:T(8,128)S(1)}) fusion(f32[1024,768]{0,1:T(8,128)S(1)} %get-tuple-element.143, f32[768]{0:T(1024)S(1)} %get-tuple-element.73, bf16[1024,768]{1,0:T(8,128)(2,1)S(1)} %bitcast.281, bf16[768,768]{1,0:T(8,128)(2,1)S(1)} %get-tuple-element.44), kind=kOutput, calls=%fused_computation.22 | convolution fusion | flops 1266941184 | bytes 10622976 | tf_op jit(solution)/shard_map/dot_general | solution.py:251
  135.5 2.9 convolution_convert_fusion.1
  138.6 4.5 %convolution_convert_fusion.2 = bf16[1024,768]{1,0:T(8,128)(2,1)} fusion(bf16[1024,768]{0,1:T(8,128)(2,1)} %get-tuple-element.86, bf16[768,768]{1,0:T(8,128)(2,1)} %copy-done.3), kind=kOutput, calls=%fused_computation.65 | convolution fusion | flops 1208745984 | bytes 4325376 | tf_op jit(solution)/shard_map/dot_general | solution.py:251
  143.1 2.5 convolution_convert_fusion.4
  145.6 36.7 %shard_map.263 = (bf16[4,256,768]{2,1,0:T(8,128)(2,1)}, bf16[4,256,768]{2,1,0:T(8,128)(2,1)}) custom-call(bf16[4,256,768]{2,1,0:T(8,128)(2,1)} %bitcast.248, bf16[4,256,768]{2,1,0:T(8,128)(2,1)} %bitcast.239), custom_call_target="tpu_custom_call" | custom-call | tf_op jit(solution)/shard_map/pallas_call | solution.py:208
  182.3 1.8 convert_reduce_fusion.6
  184.3 1.6 pad_maximum_fusion.2
  187.7 2.3 convert_reduce_fusion.13
  190.1 19.7 %shard_map.264 = bf16[4,256,768]{2,1,0:T(8,128)(2,1)} custom-call(bf16[256,768]{1,0:T(8,128)(2,1)} %get-tuple-element.89.refs_0_), custom_call_target="tpu_custom_call" | custom-call | tf_op jit(solution)/shard_map/pallas_call | solution.py:208
  209.8 2.1 convolution_convert_fusion.8
  212.0 1.5 constant_dynamic-slice_fusion
  213.4 2.0 convolution_convert_fusion.6
  216.3 6.4 %fusion.43 = f32[3,1024,1024]{1,2,0:T(8,128)} fusion(bf16[3,3,1024,64]{2,3,1,0:T(8,128)(2,1)S(1)} %bitcast.234), kind=kOutput, calls=%fused_computation.109 | convolution fusion | flops 402653184 | bytes 13369344 | tf_op jit(solution)/shard_map/hqd,hkd->hqk/dot_general | solution.py:615
  222.7 6.3 %fusion.33 = bf16[1,3,1024,64]{2,3,1,0:T(8,128)(2,1)S(1)} fusion(bf16[3,1024,64]{1,2,0:T(8,128)(2,1)S(1)} %bitcast.261, f32[3,1024,1024]{1,2,0:T(8,128)} %fusion.43, f32[3,1024]{1,0:T(4,128)S(1)} %reduce.10, pred[1024,1024]{0,1:T(8,128)(4,1)S(1)} %copy-done.8), kind=kOutput, calls=%fused_computation.78 | convolution fusion | flops 412286976 | bytes 14430208 | tf_op jit(solution)/shard_map/hqk,hqd->hkd/dot_general | solution.py:651
  229.0 11.1 %multiply_reduce_fusion = (f32[3,1024]{1,0:T(4,128)S(1)}, f32[3,1024,1024]{1,2,0:T(8,128)}) fusion(f32[3,1024,1024]{1,2,0:T(8,128)} %fusion.43, f32[3,1024]{1,0:T(4,128)S(1)} %reduce.10, pred[1024,1024]{0,1:T(8,128)(4,1)S(1)} %copy-done.8, bf16[3,1024,64]{1,2,0:T(8,128)(2,1)S(1)} %bitcast.262, bf16[3,3,1024,64]{2,3,1,0:T(8,128)(2,1)S(1)} %bitcast.235), kind=kOutput, calls=%fused_computation.1 | convolution fusion | flops 415233024 | bytes 27029504 | tf_op jit(solution)/shard_map/hqd,hkd->hqk/dot_general | solution.py:652
  240.0 1.5 copy-done.5
  241.5 7.1 %multiply_convert_fusion = bf16[3,1024,1024]{1,2,0:T(8,128)(2,1)S(1)} fusion(f32[3,1024,1024]{1,2,0:T(8,128)} %get-tuple-element.141, f32[3,1024,1024]{1,2,0:T(8,128)S(1)} %copy-done.5, f32[3,1024]{1,0:T(4,128)S(1)} %get-tuple-element.140, f32[3,1024]{1,0:T(4,128)S(1)} %reduce.10, pred[1024,1024]{0,1:T(8,128)(4,1)S(1)} %copy-done.8), kind=kLoop, calls=%fused_computation | loop fusion | flops 15728640 | bytes 32530432 | tf_op jit(solution)/shard_map/convert_element_type | solution.py:654
  248.7 2.0 fusion.36
  250.7 1.2 fusion.37
  253.1 2.9 convolution_convert_fusion.5
  255.9 2.6 convolution_convert_fusion
  258.6 19.6 %shard_map.265 = bf16[4,256,768]{2,1,0:T(8,128)(2,1)} custom-call(bf16[4,256,768]{2,1,0:T(8,128)(2,1)} %bitcast.251), custom_call_target="tpu_custom_call" | custom-call | tf_op jit(solution)/shard_map/pallas_call | solution.py:208
  278.2 2.3 convert_reduce_fusion
  280.6 1.2 pad_maximum_fusion.1.refs_0_
  284.3 52.9 %shard_map.266 = (bf16[32,48,384]{2,1,0:T(8,128)(2,1)}, bf16[32,48,384]{2,1,0:T(8,128)(2,1)}, bf16[32,48,128]{2,1,0:T(8,128)(2,1)}, bf16[32,48,384]{2,1,0:T(8,128)(2,1)}, f32[32,24,128]{2,1,0:T(8,128)}) custom-call(bf16[32,48,384]{2,1,0:T(8,128)(2,1)} %pad_maximum_fusion.1.refs_0_, bf16[32,48,384]{2,1,0:T(8,128)(2,1)} %get-tuple-element.145.refs_1_, ...), custom_call_target="tpu_custom_call" | custom-call | tf_op jit(solution)/shard_map/pallas_call | solution.py:208
  337.3 1.6 convert_reduce_fusion.9
  338.8 1.4 convert_reduce_fusion.8
  343.7 20.0 %shard_map.267 = (bf16[4,2,48,384]{3,2,1,0:T(8,128)(2,1)}, bf16[4,2,48,384]{3,2,1,0:T(8,128)(2,1)}, bf16[4,2,48,128]{3,2,1,0:T(8,128)(2,1)}, bf16[4,2,48,384]{3,2,1,0:T(8,128)(2,1)}, f32[4,24,128]{2,1,0:T(8,128)}) custom-call(bf16[2,48,384]{2,1,0:T(8,128)(2,1)} %pad_maximum_fusion.12.refs_0_, bf16[2,48,384]{2,1,0:T(8,128)(2,1)} %pad_maximum_fusion.13.refs_1_, ...), custom_call_target="tpu_custom_call" | custom-call | tf_op jit(solution)/shard_map/pallas_call | solution.py:208
  371.4 1.1 reshape.266
  372.6 1.2 copy.160
  373.8 2.6 reshape.267
  (154 shorter events, 27.4 us)
Async XLA Ops:
  0.6 5.5 %copy-start.21 = (bf16[24,3072]{1,0:T(8,128)(2,1)S(1)}, bf16[24,3072]{1,0:T(8,128)(2,1)}, u32[]{:S(2)}) copy-start(bf16[24,3072]{1,0:T(8,128)(2,1)} %param.23) | copy-start | bytes 442372
  5.1 5.1 %copy-start = (bf16[256,768]{1,0:T(8,128)(2,1)S(1)}, bf16[256,768]{1,0:T(8,128)(2,1)}, u32[]{:S(2)}) copy-start(bf16[256,768]{1,0:T(8,128)(2,1)} %src_dy.1) | copy-start | bytes 1179652
  5.1 5.1 %copy-start.1 = (bf16[256,768]{1,0:T(8,128)(2,1)S(1)}, bf16[256,768]{1,0:T(8,128)(2,1)}, u32[]{:S(2)}) copy-start(bf16[256,768]{1,0:T(8,128)(2,1)} %src_x.1) | copy-start | bytes 1179652
  80.9 1.0 copy-start.2
  82.0 1.0 copy-start.3
  111.6 1.7 copy-start.6
  112.2 1.7 copy-start.4
  114.0 8.1 %copy-start.10 = (f32[1024,768]{1,0:T(8,128)}, f32[1024,768]{1,0:T(8,128)S(1)}, u32[]{:S(2)}) copy-start(f32[1024,768]{1,0:T(8,128)S(1)} %subtract_multiply_fusion) | copy-start | bytes 9437188
  114.0 8.1 %copy-start.22 = (bf16[4,256,768]{2,1,0:T(8,128)(2,1)S(1)}, bf16[4,256,768]{2,1,0:T(8,128)(2,1)}, u32[]{:S(2)}) copy-start(bf16[4,256,768]{2,1,0:T(8,128)(2,1)} %get-tuple-element.43) | copy-start | bytes 4718596
  138.5 4.5 %copy-start.11 = (f32[1024,768]{1,0:T(8,128)S(1)}, f32[1024,768]{1,0:T(8,128)}, u32[]{:S(2)}) copy-start(f32[1024,768]{1,0:T(8,128)} %copy-done.10) | copy-start | bytes 9437188
  138.6 4.5 %copy-start.23 = (bf16[1024,768]{0,1:T(8,128)(2,1)S(1)}, bf16[1024,768]{0,1:T(8,128)(2,1)}, u32[]{:S(2)}) copy-start(bf16[1024,768]{0,1:T(8,128)(2,1)} %get-tuple-element.86) | copy-start | bytes 4718596
  182.3 1.8 copy-start.16
  182.3 2.0 copy-start.13
  184.2 1.8 copy-start.14
  184.3 3.1 copy-start.12
  211.9 4.3 %copy-start.7 = (bf16[1024,3,192]{0,2,1:T(8,128)(2,1)S(1)}, bf16[1024,3,192]{0,2,1:T(8,128)(2,1)}, u32[]{:S(2)}) copy-start(bf16[1024,3,192]{0,2,1:T(8,128)(2,1)} %slice.254) | copy-start | bytes 3538948
  216.3 6.4 %copy-start.8 = (pred[1024,1024]{0,1:T(8,128)(4,1)S(1)}, pred[1024,1024]{0,1:T(8,128)(4,1)}, u32[]{:S(2)}) copy-start(pred[1024,1024]{0,1:T(8,128)(4,1)} %iota_compare_fusion) | copy-start | bytes 3145732
  229.0 12.5 %copy-start.5 = (f32[3,1024,1024]{1,2,0:T(8,128)S(1)}, f32[3,1024,1024]{1,2,0:T(8,128)}, u32[]{:S(2)}) copy-start(f32[3,1024,1024]{1,2,0:T(8,128)} %fusion.43) | copy-start | bytes 37748740
  278.2 3.6 copy-start.9
  337.2 4.4 %copy-start.18 = (f32[32,24,128]{2,1,0:T(8,128)S(1)}, f32[32,24,128]{2,1,0:T(8,128)}, u32[]{:S(2)}) copy-start(f32[32,24,128]{2,1,0:T(8,128)} %get-tuple-element.55) | copy-start | bytes 1179652
  337.2 5.0 %copy-start.17 = (bf16[32,48,128]{2,1,0:T(8,128)(2,1)S(1)}, bf16[32,48,128]{2,1,0:T(8,128)(2,1)}, u32[]{:S(2)}) copy-start(bf16[32,48,128]{2,1,0:T(8,128)(2,1)} %get-tuple-element.53) | copy-start | bytes 1179652
  337.2 5.7 %copy-start.15 = (bf16[32,48,384]{2,1,0:T(8,128)(2,1)S(1)}, bf16[32,48,384]{2,1,0:T(8,128)(2,1)}, u32[]{:S(2)}) copy-start(bf16[32,48,384]{2,1,0:T(8,128)(2,1)} %get-tuple-element.54) | copy-start | bytes 3538948
  367.9 2.5 copy-start.20
  369.0 1.5 copy-start.19
where the time goes:
time: 381 us; the launch traced here: 377 us
  Pallas kernels  220 us (58%)
  matrix products  71.4 us (19%)
  local copies, waits for them, and re-layouts  41.9 us (11%)
  other arithmetic  41.9 us (11%)
    pallas_call x5, Pallas kernels, exchange(): pl.pallas_call(functools.partial(exchange_kernel, kinds), out_shape=shape...  149 us
    pallas_call x1, Pallas kernels, forward(): pl.pallas_call(forward_kernel, out_shape=outs, in_specs=[any_space] * 5,...  70.7 us
    dot_general x4, matrix products, dot_t(): lax.dot_general(a, b, (((1,), (1,)), ((), ())), preferred_element_type=jn...  20.2 us
    dot_general x3, matrix products, dot(): return jnp.dot(a, b, preferred_element_type=jnp.float32)  15.4 us
    dot_general x1, matrix products, on_device(): jnp.einsum('hqd,hkd->hqk', d_ctx_heads, values, preferred_element_type=full)  11.1 us
    dot_general x4, matrix products, t_dot(): lax.dot_general(a, b, (((0,), (0,)), ((), ())), preferred_element_type=jn...  8.77 us

commit v1 on v0

v1 whole, which is shorter than its diff:
```python
import functools
import math

import jax
import jax.numpy as jnp
from jax import lax
from jax.experimental import pallas as pl
from jax.experimental.pallas import tpu as pltpu
from jax.sharding import PartitionSpec as P

D = 768
H = 12
HD = 64
N = 32
G = 4
ROWS = 24
LEN = 1024
TOK = 256
HEADS = 3
OWN = HEADS * HD
PAD = 256
FFG = 768
epsilon = 1e-05
SCALE = 1.0 / math.sqrt(HD)
MESH = pl.DeviceIdType.MESH


def x_half(f):
    return lax.rem(f // 4, 2)


def place():
    return lax.axis_index("fsdp"), lax.axis_index("seq")


def send(src, dst, send_sem, recv_sem, f, s):
    pltpu.make_async_remote_copy(
        src_ref=src,
        dst_ref=dst,
        send_sem=send_sem,
        recv_sem=recv_sem,
        device_id=(f, s),
        device_id_type=MESH,
    ).start()


def take(ref, sem):
    pltpu.make_async_copy(ref, ref, sem).wait()


def loop(count, body):
    lax.fori_loop(0, count, lambda t, carry: (body(t), carry)[1], 0)


def greet(barrier, f, s):
    pl.semaphore_signal(barrier, inc=1, device_id=(f, s), device_id_type=MESH)


def pack(blocks):
    c = blocks.shape[-1] // 2
    return jnp.concatenate([blocks[..., :c], blocks[..., c:]], axis=-2)


def unpack(blocks):
    return jnp.concatenate([blocks[..., :ROWS, :], blocks[..., ROWS:, :]], axis=-1)


def pad_heads(blocks):
    return jnp.pad(blocks, [(0, 0)] * (blocks.ndim - 1) + [(0, PAD - OWN)])


def norm_parts(values):
    center = jnp.mean(values, axis=-1, keepdims=True)
    centered = values - center
    spread = jnp.mean(centered * centered, axis=-1, keepdims=True)
    inverse = lax.rsqrt(spread + epsilon)
    return centered * inverse, inverse


def norm_back(grad, gain, unit, inverse):
    scaled = grad * gain
    mean_one = jnp.mean(scaled, axis=-1, keepdims=True)
    mean_two = jnp.mean(scaled * unit, axis=-1, keepdims=True)
    return inverse * (scaled - mean_one - unit * mean_two)


def dot(a, b):
    return jnp.dot(a, b, preferred_element_type=jnp.float32)


def dot_t(a, b):
    return lax.dot_general(a, b, (((1,), (1,)), ((), ())), preferred_element_type=jnp.float32)


def t_dot(a, b):
    return lax.dot_general(a, b, (((0,), (0,)), ((), ())), preferred_element_type=jnp.float32)


def tile(t, size=TOK):
    return pl.ds(pl.multiple_of(t * size, size), size)


def lanes_of(h, shape):
    lane = lax.broadcasted_iota(jnp.int32, shape, 1)
    return lane < HD if h % 2 == 0 else lane >= HD


def only(h, block):
    return jnp.where(lanes_of(h, block.shape), block, jnp.zeros_like(block))


def causal(scores, offset):
    row = offset + lax.broadcasted_iota(jnp.int32, scores.shape, 0)
    col = lax.broadcasted_iota(jnp.int32, scores.shape, 1)
    return jnp.where(col <= row, scores, -1e9)


class Ring:
    def __init__(self, src, held, sends, recvs, own, order, f, s):
        self.src, self.held, self.sends, self.recvs, self.own = src, held, sends, recvs, own
        self.order, self.f, self.s = order, f, s
        self.y, self.h, self.z = f // 8, x_half(f), lax.rem(f, 4)

    def peer(self, axis, step):
        if axis == "y":
            return lax.rem(self.y + step + 4, 4) * 8 + lax.rem(self.f, 8), self.s
        return self.f - self.z + lax.rem(self.z + step + 4, 4), self.s

    def coordinate(self, axis, step):
        return lax.rem((self.y if axis == "y" else self.z) + step + 4, 4)

    def one(self, axis, step, half=None):
        i = self.coordinate(axis, step)
        halves = slice(None) if half is None else half
        return self.held.at[i, halves, self.z] if axis == "y" else self.held.at[self.y, halves, i]

    def many(self, axis, step, half=None):
        i = self.coordinate(axis, step)
        if axis == "y":
            return self.held.at[i] if half is None else self.held.at[i, half]
        rows = slice(None) if half is None else slice(2 * half, 2 * half + 2)
        return self.held.at[rows, slice(None), i]

    def push(self, block, k, peer):
        send(block, block, self.sends.at[k], self.recvs.at[k], *peer)

    def begin(self):
        mine = self.held.at[self.y, self.h, self.z]
        other = lax.rem(self.s + 2, G)
        send(
            self.src.at[other], mine, self.sends.at[0], self.recvs.at[0], self.f + 4 - 8 * self.h, other
        )
        pltpu.make_async_copy(self.src.at[self.s], mine, self.own.at[0]).start()

    def first(self):
        mine = self.held.at[self.y, self.h, self.z]
        take(mine, self.own.at[0])
        take(mine, self.recvs.at[0])
        axis = self.order[0]
        self.push(self.one(axis, 0), 1, self.peer(axis, 1))
        self.push(self.one(axis, 0), 2, self.peer(axis, -1))

    def relay(self, part, base, axis):
        take(part(axis, -1), self.recvs.at[base])
        self.push(part(axis, -1, 0), base + 2, self.peer(axis, 1))
        take(part(axis, 1), self.recvs.at[base + 1])
        self.push(part(axis, 1, 1), base + 3, self.peer(axis, -1))

    def first_relay(self):
        self.relay(self.one, 1, self.order[0])

    def last(self):
        axis = self.order[0]
        take(self.one(axis, 2, 0), self.recvs.at[3])
        take(self.one(axis, 2, 1), self.recvs.at[4])
        axis = self.order[1]
        self.push(self.many(axis, 0), 5, self.peer(axis, 1))
        self.push(self.many(axis, 0), 6, self.peer(axis, -1))

    def last_relay(self):
        self.relay(self.many, 5, self.order[1])

    def arrive(self):
        axis = self.order[1]
        take(self.many(axis, 2, 0), self.recvs.at[7])
        take(self.many(axis, 2, 1), self.recvs.at[8])

    def drain(self):
        one, many = self.order
        take(self.held.at[self.y, self.h, self.z], self.sends.at[0])
        for k in (1, 2):
            take(self.one(one, 0), self.sends.at[k])
            take(self.one(one, 0, 0), self.sends.at[k + 2])
            take(self.many(many, 0), self.sends.at[k + 4])
            take(self.many(many, 0, 0), self.sends.at[k + 6])


class Share:
    def __init__(self, block, sends, recvs, f, s):
        self.block, self.sends, self.recvs, self.f, self.s = block, sends, recvs, f, s
        self.twin = s + 1 - 2 * lax.rem(s, 2)
        self.across = lax.rem(s + 2, G)

    def begin(self):
        mine = self.block(self.s)
        send(mine, mine, self.sends.at[1], self.recvs.at[1], self.f, self.across)
        send(mine, mine, self.sends.at[0], self.recvs.at[0], self.f, self.twin)

    def relay(self):
        theirs = self.block(self.across)
        take(theirs, self.recvs.at[1])
        send(theirs, theirs, self.sends.at[2], self.recvs.at[2], self.f, self.twin)

    def arrive(self):
        take(self.block(self.s), self.recvs.at[0])
        take(self.block(self.s), self.recvs.at[2])

    def drain(self):
        for k in range(3):
            take(self.block(self.s), self.sends.at[k])


def greet_near(barrier, f, s):
    y, h, z = f // 8, x_half(f), lax.rem(f, 4)
    greet(barrier, f + 4 - 8 * h, lax.rem(s + 2, G))
    greet(barrier, f + 4 - 8 * h, s)
    for step in (1, 3):
        greet(barrier, lax.rem(y + step, 4) * 8 + lax.rem(f, 8), s)
        greet(barrier, f - z + lax.rem(z + step, 4), s)
    for step in (1, 2, 3):
        greet(barrier, f, lax.rem(s + step, G))
    pl.semaphore_wait(barrier, 9)


def unpack_rings(held, first, wide):
    c = held.shape[-1]

    def pair(p):
        at = (p // 4, lax.rem(p // 2, 2))
        z = 2 * lax.rem(p, 2)
        one = held[at[0], at[1], z, first : first + 48, :].astype(jnp.float32)
        two = held[at[0], at[1], z + 1, first : first + 48, :].astype(jnp.float32)
        rows = pl.ds(pl.multiple_of(48 * p, 48), 48)
        wide[rows, :c] = jnp.concatenate([one[:ROWS], two[:ROWS]], axis=0).astype(wide.dtype)
        wide[rows, c:] = jnp.concatenate([one[ROWS:], two[ROWS:]], axis=0).astype(wide.dtype)

    loop(N // 2, pair)


def spread_vectors(held, vec, f, s):
    low, full = jnp.bfloat16, jnp.float32
    row = lax.broadcasted_iota(jnp.int32, (128, D), 0)
    lane = lax.broadcasted_iota(jnp.int32, (128, D), 1)
    inside = lax.rem(lane, ROWS)
    plain = (row == inside).astype(full).astype(low)
    shifted = (row == inside + ROWS * s).astype(full).astype(low)
    owner = lax.broadcasted_iota(jnp.int32, (16, D), 1) // ROWS
    number = lax.broadcasted_iota(jnp.int32, (16, D), 0)
    vec[...] = jnp.zeros_like(vec)

    def add(j):
        block = held[j // 8, lax.rem(j // 4, 2), lax.rem(j, 4), 48:64, :128]
        straight, moved = dot(block, plain), dot(block, shifted)
        wanted = jnp.where(number < 7, j, jnp.where(j // 8 == s, lax.rem(j, 8), -1))
        vec[...] += jnp.where(owner == wanted, jnp.where(number == 6, moved, straight), 0.0)

    loop(N, add)


class RingSum:
    def __init__(self, part, inbox, total, sends, recvs, order, f, s):
        self.part, self.inbox, self.total = part, inbox, total
        self.sends, self.recvs, self.f, self.s = sends, recvs, f, s
        self.line = Ring(None, part, None, None, None, order, f, s)
        self.order = order

    def push(self, block, inbox, k, peer):
        send(block, inbox, self.sends.at[k], self.recvs.at[k], *peer)

    def add(self, block, *inboxes):
        total = block[...].astype(jnp.float32)
        for inbox in inboxes:
            total = total + inbox[...].astype(jnp.float32)
        block[...] = total.astype(block.dtype)

    def stage(self, section, axis, far, near, base):
        line = self.line
        self.push(section(axis, 2, 0), far.at[0], base, line.peer(axis, 1))
        self.push(section(axis, 2, 1), far.at[1], base + 1, line.peer(axis, -1))
        yield
        take(far.at[0], self.recvs.at[base])
        self.add(section(axis, 1, 0), far.at[0])
        self.push(section(axis, 1), near.at[0], base + 2, line.peer(axis, 1))
        take(far.at[1], self.recvs.at[base + 1])
        self.add(section(axis, -1, 1), far.at[1])
        self.push(section(axis, -1), near.at[1], base + 3, line.peer(axis, -1))
        yield
        take(near.at[0], self.recvs.at[base + 2])
        take(near.at[1], self.recvs.at[base + 3])
        self.add(section(axis, 0), near.at[0], near.at[1])

    def steps(self):
        line = self.line
        far_many, near_many, far_one, near_one, beyond = self.inbox
        yield from self.stage(line.many, self.order[1], far_many, near_many, 0)
        yield from self.stage(line.one, self.order[0], far_one, near_one, 4)
        self.push(
            self.part.at[line.y, 1 - line.h, line.z], beyond, 8, (self.f + 4 - 8 * line.h, self.s)
        )
        yield
        take(beyond, self.recvs.at[8])
        mine = self.part[line.y, line.h, line.z].astype(jnp.float32)
        self.total[self.s] = (mine + beyond[...].astype(jnp.float32)).astype(self.total.dtype)

    def drain(self):
        far_many, near_many, far_one, near_one, beyond = self.inbox
        for k, ref in enumerate((far_many, far_many, near_many, near_many, far_one, far_one, near_one, near_one)):
            take(ref.at[0], self.sends.at[k])
        take(beyond, self.sends.at[8])


def ring_inbox(order, rows):
    many = (4, 2) if order[1] == "z" else (2, 4)
    half = (2, 2) if order[1] == "z" else (4,)
    block = (rows, 384)
    return [(2,) + half + block, (2,) + many + block, (2,) + block, (2, 2) + block, block]


class SeqSum:
    def __init__(self, part, twins, crossed, sends, recvs, f, s):
        self.part, self.twins, self.crossed = part, twins, crossed
        self.sends, self.recvs, self.f, self.s = sends, recvs, f, s
        self.twin = s + 1 - 2 * lax.rem(s, 2)
        self.across = lax.rem(s + 2, G)
        self.far_twin = 3 - s

    def ready(self, t):
        @pl.when(t == self.far_twin)
        def _():
            send(
                self.part.at[self.far_twin], self.twins.at[0], self.sends.at[0], self.recvs.at[0], self.f, self.twin
            )

        @pl.when(t == self.twin)
        def _():
            send(self.part.at[self.twin], self.twins.at[1], self.sends.at[2], self.recvs.at[2], self.f, self.twin)

    def relay(self, t):
        @pl.when(t == self.across)
        def _():
            take(self.twins.at[0], self.recvs.at[0])
            both = self.part[self.across].astype(jnp.float32) + self.twins[0].astype(jnp.float32)
            self.part[self.across] = both.astype(self.part.dtype)
            send(
                self.part.at[self.across], self.crossed, self.sends.at[1], self.recvs.at[1], self.f, self.across
            )

    def total(self):
        take(self.crossed, self.recvs.at[1])
        take(self.crossed, self.recvs.at[2])
        mine = self.part[self.s].astype(jnp.float32) + self.twins[1].astype(jnp.float32)
        return mine + self.crossed[...].astype(jnp.float32)

    def drain(self):
        for k in range(3):
            take(self.crossed, self.sends.at[k])


def cut_grad(left, right, part, first, chunks):
    low = part.dtype

    def chunk(c):
        columns = pl.ds(pl.multiple_of(c * 384, 128), 384)
        made = t_dot(left[:, columns], right[...])
        for i in range(16):
            block = made[i * ROWS : (i + 1) * ROWS]
            packed = jnp.concatenate([block[:, :384], block[:, 384:]], axis=0).astype(low)
            part[2 * c + i // 8, (i // 4) % 2, i % 4, first : first + 48, :] = packed

    loop(chunks, chunk)


def column_sum(values):
    return jnp.sum(values, axis=0, keepdims=True)


RING_PLAN = (("yz", 48), ("zy", 48), ("yz", 16), ("yz", 32), ("zy", 32))


def layer_kernel(*refs):
    (
        src_a, src_b, src_c, src_x, src_dy,
        output, grad_input, fin_up, fin_down, fin_out, fin_a, fin_b,
        got_x, vec, normed, qkv, w_in, lse, got_ctx, w_out, w_up, w_down, got_dy,
        held_a, held_b, held_c,
        residual, normed_two, active, d_hidden, branch, d_ctx, d_proj, d_key, d_value, d_res, sums, grad_in,
        out_part, out_twins, out_crossed, two_part, two_twins, two_crossed, one_part, one_twins, one_crossed,
        part_up, part_down, part_out, part_a, part_b,
        *inboxes,
        ring_ss, ring_rs, ring_own, seq_ss, seq_rs, seq_own, sum_ss, sum_rs, part_ss, part_rs,
    ) = refs
    low, full = jnp.bfloat16, jnp.float32
    f, s = place()
    greet_near(pltpu.get_barrier_semaphore(), f, s)
    ring_a, ring_b, ring_c = [
        Ring(src, held, ring_ss.at[k], ring_rs.at[k], ring_own.at[k], order, f, s)
        for k, (src, held, order) in enumerate(
            ((src_a, held_a, "yz"), (src_b, held_b, "zy"), (src_c, held_c, "yz"))
        )
    ]
    rings = (ring_a, ring_b, ring_c)
    copies = [
        pltpu.make_async_copy(src, dst.at[s], seq_own.at[k])
        for k, (src, dst) in enumerate(((src_x, got_x), (src_dy, got_dy)))
    ]
    for copy in copies:
        copy.start()
    for ring in rings:
        ring.begin()
    share_x, share_dy = [
        Share(lambda i, dst=dst: dst.at[i], seq_ss.at[k], seq_rs.at[k], f, s)
        for k, dst in enumerate((got_x, got_dy))
    ]
    copies[0].wait()
    share_x.begin()
    for ring in rings:
        ring.first()
    for ring in rings:
        ring.first_relay()
    for ring in rings:
        ring.last()
    share_x.relay()
    copies[1].wait()
    share_dy.begin()
    share_x.arrive()
    for ring in rings:
        ring.last_relay()
    ring_a.arrive()
    spread_vectors(held_a, vec, f, s)
    gain, shift = vec[0:1, :], vec[1:2, :]

    def norm_tile(t):
        unit, _ = norm_parts(got_x[t].astype(jnp.float32))
        normed[tile(t), :] = (unit * gain + shift).astype(normed.dtype)

    loop(G, norm_tile)
    unpack_rings(held_a, 0, w_in)
    bias = jnp.concatenate([vec[7:8, :PAD], jnp.zeros((1, PAD), jnp.float32), vec[8:9, :PAD]], axis=1)

    def project(t):
        made = (dot(normed[tile(t), :], w_in[...]) + bias).astype(qkv.dtype)
        qkv[tile(t), :PAD] = (made[:, :PAD].astype(jnp.float32) * SCALE).astype(qkv.dtype)
        qkv[tile(t), PAD:] = made[:, PAD:]

    loop(G, project)
    share_dy.relay()
    shares = []
    for step, b in enumerate((3, 2, 1, 0)):
        rows, span = slice(b * TOK, (b + 1) * TOK), (b + 1) * TOK
        for pair in range(2):
            at = pair * 128
            made = None
            for h in range(2 * pair, min(2 * pair + 2, HEADS)):
                query = only(h, qkv[rows, at : at + 128])
                scores = causal(dot_t(query, qkv[:span, PAD + at : PAD + at + 128]), b * TOK)
                peak = jnp.max(scores, axis=-1, keepdims=True)
                weights = jnp.exp(scores - peak)
                total = jnp.sum(weights, axis=-1, keepdims=True)
                lse[h, rows, :] = peak + jnp.log(total)
                part = dot(weights.astype(qkv.dtype), qkv[:span, 2 * PAD + at : 2 * PAD + at + 128]) / total
                made = part if made is None else jnp.where(lanes_of(h, part.shape), part, made)
            got_ctx[s, rows, at : at + 128] = made.astype(got_ctx.dtype)
        shares.append(
            Share(
                lambda i, b=b: got_ctx.at[i, pl.ds(b * TOK, TOK)], seq_ss.at[2 + step], seq_rs.at[2 + step], f, s
            )
        )
        shares[-1].begin()
        if step:
            shares[step - 1].relay()
    shares[-1].relay()
    ring_b.arrive()
    unpack_rings(held_b, 0, w_out)
    unpack_rings(held_b, 48, w_up)
    ring_c.arrive()
    unpack_rings(held_c, 0, w_down)
    share_dy.arrive()
    for share in shares:
        share.arrive()

    sum_out = SeqSum(out_part, out_twins, out_crossed, part_ss.at[0], part_rs.at[0], f, s)
    sum_two = SeqSum(two_part, two_twins, two_crossed, part_ss.at[1], part_rs.at[1], f, s)
    sum_one = SeqSum(one_part, one_twins, one_crossed, part_ss.at[2], part_rs.at[2], f, s)
    sums[...] = jnp.zeros_like(sums)
    gain_two, shift_two = vec[2:3, :], vec[3:4, :]

    def turn(i):
        return jnp.where(i == 0, 3 - s, jnp.where(i == 1, lax.rem(s + 2, G), jnp.where(i == 2, sum_two.twin, s)))

    def feed(i):
        t = turn(i)
        rows = tile(t)
        value = got_x[t].astype(full) + vec[4:5, :]
        for g in range(G):
            value = value + dot(got_ctx[g, rows, :OWN], w_out[g * OWN : (g + 1) * OWN, :])
        residual[rows, :] = value
        unit, _ = norm_parts(value)
        normed_low = (unit * gain_two + shift_two).astype(low)
        normed_two[rows, :] = normed_low
        hidden = dot(normed_low, w_up[...]) + vec[6:7, :]
        cdf = 0.5 * (1.0 + lax.erf(hidden * math.sqrt(0.5)))
        active_low = (hidden * cdf).astype(low)
        active[rows, :] = active_low
        slope = cdf + hidden * jnp.exp(-0.5 * hidden * hidden) * (1.0 / math.sqrt(2.0 * math.pi))
        dy = got_dy[t]
        d_low = (dot_t(dy, w_down[...]) * slope).astype(low)
        d_hidden[rows, :] = d_low
        d_two = dot_t(d_low, w_up[...])
        two_part[t] = d_two.astype(low)
        sum_two.ready(t)
        sums[2:3, :] += column_sum(d_two * unit)
        sums[3:4, :] += column_sum(d_two)
        sums[8:9, :] += column_sum(d_low.astype(full))
        out_part[t] = dot(active_low, w_down[...]).astype(low)
        sum_out.ready(t)

        @pl.when(i > 1)
        def _():
            sum_two.relay(turn(i - 1))
            sum_out.relay(turn(i - 1))

    loop(G, feed)

    inbox = [inboxes[5 * k : 5 * k + 5] for k in range(5)]
    totals = (fin_up, fin_down, fin_out, fin_a, fin_b)
    parts = (part_up, part_down, part_out, part_a, part_b)
    adders = [
        RingSum(parts[k], inbox[k], totals[k], sum_ss.at[k], sum_rs.at[k], RING_PLAN[k][0], f, s) for k in range(5)
    ]
    finals = [
        Share(lambda i, k=k: totals[k].at[i], seq_ss.at[7 + k], seq_rs.at[7 + k], f, s) for k in range(5)
    ]

    def life(k):
        yield from adders[k].steps()
        finals[k].begin()
        yield
        finals[k].relay()
        yield
        finals[k].arrive()

    lives = [life(k) for k in range(5)]

    def advance(*which):
        for k in which:
            next(lives[k], None)

    cut_grad(normed_two, d_hidden, part_up, 0, 2)
    advance(0)
    flat_dy = [got_dy[t] for t in range(G)]
    dy_all = jnp.concatenate(flat_dy, axis=0)

    def chunk_down(c):
        columns = pl.ds(pl.multiple_of(c * 384, 128), 384)
        made = t_dot(active[:, columns], dy_all)
        for i in range(16):
            block = made[i * ROWS : (i + 1) * ROWS]
            packed = jnp.concatenate([block[:, :384], block[:, 384:]], axis=0).astype(low)
            part_down[2 * c + i // 8, (i // 4) % 2, i % 4] = packed

    loop(2, chunk_down)
    advance(1)

    mine = tile(s)
    own_res = residual[mine, :]
    unit, inverse = norm_parts(own_res)
    own_dy = got_dy[s].astype(full)
    d_own = own_dy + norm_back(sum_two.total(), gain_two, unit, inverse)
    d_res[...] = d_own
    branch[s] = d_own.astype(low)
    share_branch = Share(lambda i: branch.at[i], seq_ss.at[6], seq_rs.at[6], f, s)
    share_branch.begin()
    sums[4:5, :] += column_sum(d_own.astype(low).astype(full))
    sums[5:6, :] += column_sum(own_dy)
    advance(0, 1)
    share_branch.relay()
    output[...] = (own_res + sum_out.total() + vec[5:6, :]).astype(low)
    d_key[...] = jnp.zeros_like(d_key)
    d_value[...] = jnp.zeros_like(d_value)
    share_branch.arrive()

    own_rows = pl.ds(pl.multiple_of(s * OWN, 64), OWN)
    pick = lax.broadcasted_iota(jnp.int32, (D, PAD), 0) == lax.broadcasted_iota(jnp.int32, (D, PAD), 1) + s * OWN
    pick = jnp.logical_and(pick, lax.broadcasted_iota(jnp.int32, (D, PAD), 1) < OWN)
    pick = pick.astype(full).astype(low)
    picked = [dot(branch[t], pick).astype(low) for t in range(G)]
    picked = jnp.concatenate(picked, axis=0)

    def cut_out(g):
        made = t_dot(got_ctx[g], picked)
        for i in range(8):
            one, two, three = [made[i * ROWS + 8 * r : i * ROWS + 8 * r + 8] for r in range(3)]
            upper = jnp.concatenate([one, two[:, :128]], axis=1)
            lower = jnp.concatenate([two[:, 128:], three], axis=1)
            part_out[g, i // 4, i % 4] = jnp.concatenate([upper, lower], axis=0).astype(low)

    loop(G, cut_out)
    advance(2)
    for b in (3, 2, 1, 0):
        rows, span = slice(b * TOK, (b + 1) * TOK), (b + 1) * TOK
        made = dot_t(branch[b], w_out[own_rows, :])
        d_block = jnp.concatenate([made, jnp.zeros((TOK, PAD - OWN), full)], axis=1).astype(low)
        for pair in range(2):
            at = pair * 128
            d_query = None
            for h in range(2 * pair, min(2 * pair + 2, HEADS)):
                query = only(h, qkv[rows, at : at + 128])
                key = qkv[:span, PAD + at : PAD + at + 128]
                grad = only(h, d_block[:, at : at + 128])
                probs = jnp.exp(causal(dot_t(query, key), b * TOK) - lse[h, rows, :])
                d_value[:span, at : at + 128] += t_dot(probs.astype(low), grad)
                d_probs = dot_t(grad, qkv[:span, 2 * PAD + at : 2 * PAD + at + 128])
                inner = jnp.sum(probs * d_probs, axis=-1, keepdims=True)
                d_scores = (probs * (d_probs - inner)).astype(low)
                d_key[:span, at : at + 128] += t_dot(d_scores, query)
                part = dot(d_scores, key) * SCALE
                d_query = part if d_query is None else jnp.where(lanes_of(h, part.shape), part, d_query)
            if pair:
                d_query = only(0, d_query)
            d_proj[rows, at : at + 128] = d_query.astype(low)
            advance(0, 1, 2)
        d_proj[rows, PAD : 2 * PAD] = d_key[rows, :].astype(low)
        d_proj[rows, 2 * PAD :] = d_value[rows, :].astype(low)
        d_one = dot_t(d_proj[rows, :], w_in[...])
        one_part[b] = d_one.astype(low)
        sum_one.ready(b)
        unit, _ = norm_parts(got_x[b].astype(full))
        sums[0:1, :] += column_sum(d_one * unit)
        sums[1:2, :] += column_sum(d_one)
        if b < 3:
            sum_one.relay(b + 1)
    sum_one.relay(0)

    sums[6:7, :PAD] = column_sum(d_proj[:, :PAD].astype(full))
    sums[7:8, :PAD] = column_sum(d_proj[:, 2 * PAD :].astype(full))
    lane = lax.broadcasted_iota(jnp.int32, (16, D), 1) // ROWS
    number = lax.broadcasted_iota(jnp.int32, (16, D), 0)
    up_row = jnp.broadcast_to(sums[8:9, :], (16, D))
    plain = jnp.where(number < 8, sums[...], jnp.where(number == 8 + s, up_row, 0.0))
    compact = lax.rem(lax.broadcasted_iota(jnp.int32, (D, 128), 0), ROWS) == lax.broadcasted_iota(
        jnp.int32, (D, 128), 1
    )
    compact = compact.astype(full).astype(low)
    pad_lanes = jnp.zeros((16, 256), low)

    def cut_in(c):
        columns = pl.ds(pl.multiple_of(c * 384, 128), 384)
        made = t_dot(normed[:, columns], d_proj[...])
        for i in range(16):
            block = made[i * ROWS : (i + 1) * ROWS]
            packed = jnp.concatenate([block[:, :384], block[:, 384:]], axis=0)
            at = (2 * c + i // 8, (i // 4) % 2, i % 4)
            part_a[at[0], at[1], at[2]] = packed[:32].astype(low)
            part_b[at[0], at[1], at[2], :16, :] = packed[32:].astype(low)
            owner = 16 * c + i
            wanted = jnp.where(jnp.logical_or(number == 6, number == 7), owner - 8 * s, owner)
            few = dot(jnp.where(lane == wanted, plain, 0.0).astype(low), compact).astype(low)
            part_b[at[0], at[1], at[2], 16:, :] = jnp.concatenate([few, pad_lanes], axis=1)

    loop(2, cut_in)
    advance(3, 4)
    advance(0, 1, 2)
    unit, inverse = norm_parts(got_x[s].astype(full))
    grad_input[...] = (d_res[...] + norm_back(sum_one.total(), gain, unit, inverse)).astype(low)
    for _ in range(8):
        advance(3, 4)
    for k in (0, 1, 2, 3, 4):
        for _ in lives[k]:
            pass
    for share in [share_x, share_dy, share_branch] + shares + finals:
        share.drain()
    for ring in rings:
        ring.drain()
    for adder in adders + [sum_out, sum_two, sum_one]:
        adder.drain()


def layer(src_a, src_b, src_c, inputs, cotangent):
    low, full = jnp.bfloat16, jnp.float32
    any_space, vmem = pl.BlockSpec(memory_space=pl.ANY), pl.BlockSpec(memory_space=pltpu.VMEM)
    outs = [jax.ShapeDtypeStruct((TOK, D), low)] * 2
    outs += [jax.ShapeDtypeStruct((G, rows, 384), low) for _, rows in RING_PLAN]
    seq_part = [pltpu.VMEM((G, TOK, D), low), pltpu.VMEM((2, TOK, D), low), pltpu.VMEM((TOK, D), low)]
    return pl.pallas_call(
        layer_kernel,
        out_shape=outs,
        in_specs=[any_space] * 5,
        out_specs=[vmem] * len(outs),
        scratch_shapes=[
            pltpu.VMEM((G, TOK, D), low),
            pltpu.VMEM((16, D), full),
            pltpu.VMEM((LEN, D), low),
            pltpu.VMEM((LEN, 3 * PAD), low),
            pltpu.VMEM((D, 3 * PAD), low),
            pltpu.VMEM((HEADS, LEN, 1), full),
            pltpu.VMEM((G, LEN, PAD), low),
            pltpu.VMEM((D, D), low),
            pltpu.VMEM((D, FFG), low),
            pltpu.VMEM((FFG, D), low),
            pltpu.VMEM((G, TOK, D), low),
        ]
        + [pltpu.VMEM((4, 2, 4, rows, 384), low) for rows in (64, 96, 48)]
        + [
            pltpu.VMEM((LEN, D), full),
            pltpu.VMEM((LEN, D), low),
            pltpu.VMEM((LEN, FFG), low),
            pltpu.VMEM((LEN, FFG), low),
            pltpu.VMEM((G, TOK, D), low),
            pltpu.VMEM((16, PAD), low),
            pltpu.VMEM((LEN, 3 * PAD), low),
            pltpu.VMEM((LEN, PAD), full),
            pltpu.VMEM((LEN, PAD), full),
            pltpu.VMEM((TOK, D), full),
            pltpu.VMEM((16, D), full),
            pltpu.VMEM((16, D), full),
        ]
        + seq_part * 3
        + [pltpu.VMEM((4, 2, 4, rows, 384), low) for _, rows in RING_PLAN]
        + [pltpu.VMEM(shape, low) for order, rows in RING_PLAN for shape in ring_inbox(order, rows)]
        + [pltpu.SemaphoreType.DMA((3, 9))] * 2
        + [pltpu.SemaphoreType.DMA((3, 1))]
        + [pltpu.SemaphoreType.DMA((12, 3))] * 2
        + [pltpu.SemaphoreType.DMA((2,))]
        + [pltpu.SemaphoreType.DMA((5, 9))] * 2
        + [pltpu.SemaphoreType.DMA((3, 3))] * 2,
        compiler_params=pltpu.CompilerParams(
            collective_id=0, has_side_effects=True, vmem_limit_bytes=62 * 2**20
        ),
    )(src_a, src_b, src_c, inputs, cotangent)


def on_device(
    inputs,
    proj_in,
    bias_query,
    bias_value,
    proj_out,
    bias_out,
    norm_gain,
    norm_shift,
    up_weight,
    up_bias,
    down_weight,
    down_bias,
    post_gain,
    post_shift,
    cotangent,
):
    low = jnp.bfloat16
    full = jnp.float32
    f, s = place()
    split = proj_in.reshape(ROWS, 3, G, OWN).transpose(2, 0, 1, 3)
    send_in = pack(pad_heads(split).reshape(G, ROWS, 3 * PAD))
    units = up_weight.reshape(ROWS, N, G, ROWS).transpose(2, 0, 1, 3).reshape(G, ROWS, FFG)
    send_out = jnp.broadcast_to(pack(proj_out)[None], (G, 48, 384))
    vectors = jnp.stack(
        [norm_gain, norm_shift, post_gain, post_shift, bias_out, down_bias, jnp.zeros_like(bias_out), bias_query, bias_value]
    )
    compact = jnp.pad(vectors, ((0, 7), (0, 384 - ROWS)))
    compact = compact + jnp.pad(up_bias[None], ((6, 9), (0, 384 - 96)))
    src_a = jnp.concatenate([send_in, jnp.broadcast_to(compact[None], (G, 16, 384))], axis=1)
    src_b = jnp.concatenate([send_out, pack(units)], axis=1)
    src_c = pack(down_weight.reshape(G, ROWS, D))
    output, grad_input, all_up, all_down, all_out, all_a, all_b = layer(src_a, src_b, src_c, inputs, cotangent)
    split_in = jnp.concatenate([all_a, all_b[:, :16]], axis=1)
    final_in = unpack(split_in.astype(full)).reshape(G, ROWS, 3, PAD)[..., :OWN].transpose(1, 2, 0, 3)
    final_up = unpack(all_up.astype(full)).reshape(G, ROWS, N, ROWS).transpose(1, 2, 0, 3).reshape(ROWS, G * FFG)
    upper, lower = all_out[:, :8].astype(full), all_out[:, 8:].astype(full)
    second = jnp.concatenate([upper[..., PAD:], lower[..., :128]], axis=-1)
    out_blocks = jnp.concatenate([upper[..., :PAD], second, lower[..., 128:]], axis=1)
    final_out = out_blocks[..., :OWN].transpose(1, 0, 2).reshape(ROWS, D)
    final_down = unpack(all_down.astype(full)).reshape(96, D)
    final_vec = jnp.sum(all_b[:, 16:, :ROWS].astype(full), axis=0)
    return (
        output,
        grad_input,
        final_in.reshape(ROWS, 3 * D),
        final_vec[6],
        final_vec[7],
        final_out,
        final_vec[4],
        final_vec[0],
        final_vec[1],
        final_up,
        final_vec[8:12].reshape(96),
        final_down,
        final_vec[5],
        final_vec[2],
        final_vec[3],
    )


def solution(mesh):
    rows, wide, flat = P(("fsdp", "seq"), None), P("fsdp", None), P("fsdp")
    return jax.shard_map(
        on_device,
        mesh=mesh,
        in_specs=(rows, wide, flat, flat, wide, flat, flat, flat, wide, flat, wide, flat, flat, flat, rows),
        out_specs=(rows, rows, wide, flat, flat, wide, flat, flat, flat, wide, flat, wide, flat, flat, flat),
        check_vma=False,
    )
```

time: 381 us -> 183 us (0.48)
  matrix products: 71.4 us -> 0 us
  Pallas kernels: 220 us -> 162 us
  other arithmetic: 41.9 us -> 3.72 us
  local copies, waits for them, and re-layouts: 41.9 us -> 15.7 us
    dot_general x16 -> x0, matrix products: 71.4 us -> none  [the longest x4 20.2 us: dot_t(): lax.dot_general(a, b, (((1,), (1,)), ((), ())), preferred_element_type=jn...]
    pallas_call x6 -> x1, Pallas kernels: 220 us -> 162 us  [layer(): pl.pallas_call(layer_kernel, out_shape=outs, in_specs=[any_space] * 5, ou...]
    reduce_sum x16 -> x1, other arithmetic: 16.8 us -> 0.01 us  [on_device(): final_vec = jnp.sum(all_b[:, 16:, :ROWS].astype(full), axis=0)]
    convert_element_type x7 -> x2, other arithmetic: 13.6 us -> 0.79 us  [the longest x1 0.77 us: on_device(): upper, lower = (all_out[:, :8].astype(full), all_out[:, 8:].astype(full))]
    transpose x8 -> x4, local copies, waits for them, and re-layouts: 9.43 us -> 1.55 us  [the longest x1 1.25 us: on_device(): unpack(all_up.astype(full)).reshape(G, ROWS, N, ROWS).transpose(1, 2, 0, 3)]
    unnamed x51 -> x32, local copies, waits for them, and re-layouts: 5.89 us -> 1.58 us
where the time goes in v1:
time: 183 us; the launch traced here: 182 us
  Pallas kernels  162 us (89%)
  local copies, waits for them, and re-layouts  15.7 us (9%)
  other arithmetic  3.72 us (2%)
    pallas_call x1, Pallas kernels, layer(): pl.pallas_call(layer_kernel, out_shape=outs, in_specs=[any_space] * 5, ou...  162 us
    reshape x2, local copies, waits for them, and re-layouts, on_device(): unpack(all_up.astype(full)).reshape(G, ROWS, N, ROWS).transpose(1, 2, 0, 3)  3.68 us

profile of v1, /device:TPU:1, one launch (start us, length us, event | category | flops | bytes accessed | tf_op | source)
XLA Modules:
  0.0 182.4 jit_solution(13521664529563783865)
XLA Ops:
  0.6 0.7 fusion.7
  1.4 2.1 %reshape.70 = bf16[24,32,4,24]{3,2,1,0:T(4,128)(2,1)S(1)} reshape(bf16[24,3072]{1,0:T(8,128)(2,1)} %param.23) | data formatting | bytes 294912 | tf_op jit(solution)/shard_map/reshape | solution.py:764
  3.5 0.0 copy-start.3
  3.6 0.1 copy.39
  3.7 0.0 copy-start.6
  3.7 0.0 copy-start.7
  3.7 0.0 copy-start.8
  3.7 0.0 copy-start.9
  3.7 0.0 copy-start.10
  3.8 0.0 copy-start.11
  3.8 0.0 copy-start.12
  3.8 0.0 copy-start.13
  3.8 0.0 copy-start.14
  3.8 1.2 reshape.71
  5.0 0.0 copy-start.2
  5.1 0.7 pad_maximum_fusion.refs_1_
  5.8 0.0 copy-done.3
  5.8 0.2 reshape.68
  6.0 0.1 copy.44
  6.1 0.1 pad.12
  6.2 0.2 reshape.69
  6.4 0.0 copy-done.6
  6.4 0.0 copy-done.7
  6.5 0.1 stack.35
  6.5 0.0 copy-done.14
  6.6 0.7 pad_maximum_fusion.4.refs_0_
  7.3 0.7 pad_maximum_fusion.5.refs_2_
  8.0 161.9 %shard_map.262 = (bf16[256,768]{1,0:T(8,128)(2,1)}, bf16[256,768]{1,0:T(8,128)(2,1)}, bf16[4,48,384]{2,1,0:T(8,128)(2,1)}, bf16[4,48,384]{2,1,0:T(8,128)(2,1)}, ...) custom-call(bf16[4,64,384]{2,1,0:T(8,128)(2,1)} %pad_maximum_fusion.4.refs_0_, ...), custom_call_target="tpu_custom_call" | custom-call | tf_op jit(solution)/shard_map/pallas_call | solution.py:694
  169.9 0.8 slice_convert_fusion.1
  170.8 0.7 reshape.75
  171.5 1.0 fusion.2
  172.6 0.7 pad_maximum_fusion.3
  173.3 1.1 reshape.76
  174.4 1.2 copy.42
  175.7 0.0 copy-start.5
  175.7 0.0 copy-start.4
  175.7 2.5 %reshape.77 = f32[24,3072]{1,0:T(8,128)} reshape(f32[24,32,4,24]{3,2,1,0:T(4,128)S(1)} %copy.42) | data formatting | bytes 589824 | tf_op jit(solution)/shard_map/reshape | solution.py:777
  178.3 0.0 copy-done.5
  178.3 0.0 copy-done.4
  178.4 0.0 copy-start.1
  178.4 0.2 reshape.73
  178.6 0.1 slice_bitcast_fusion
  178.6 0.2 copy.40
  178.8 0.9 reshape.74
  179.7 0.5 slice_bitcast_fusion.1
  180.3 0.6 reshape.78
  180.9 0.7 copy.47
  181.6 0.7 copy.48
  (31 shorter events, 0.3 us)
Async XLA Ops:
  3.5 2.3 %copy-start.3 = (bf16[24,2304]{1,0:T(8,128)(2,1)S(1)}, bf16[24,2304]{1,0:T(8,128)(2,1)}, u32[]{:S(2)}) copy-start(bf16[24,2304]{1,0:T(8,128)(2,1)} %param.16) | copy-start | bytes 331780
  3.7 2.7 %copy-start.6 = (bf16[24]{0:T(256)(128)(2,1)S(1)}, bf16[24]{0:T(256)(128)(2,1)}, u32[]{:S(2)}) copy-start(bf16[24]{0:T(256)(128)(2,1)} %param.21) | copy-start | bytes 148
  3.7 2.7 %copy-start.7 = (bf16[24]{0:T(256)(128)(2,1)S(1)}, bf16[24]{0:T(256)(128)(2,1)}, u32[]{:S(2)}) copy-start(bf16[24]{0:T(256)(128)(2,1)} %param.22) | copy-start | bytes 148
  3.7 2.7 %copy-start.8 = (bf16[24]{0:T(256)(128)(2,1)S(1)}, bf16[24]{0:T(256)(128)(2,1)}, u32[]{:S(2)}) copy-start(bf16[24]{0:T(256)(128)(2,1)} %param.27) | copy-start | bytes 148
  3.7 2.7 %copy-start.9 = (bf16[24]{0:T(256)(128)(2,1)S(1)}, bf16[24]{0:T(256)(128)(2,1)}, u32[]{:S(2)}) copy-start(bf16[24]{0:T(256)(128)(2,1)} %param.28) | copy-start | bytes 148
  3.7 2.7 %copy-start.10 = (bf16[24]{0:T(256)(128)(2,1)S(1)}, bf16[24]{0:T(256)(128)(2,1)}, u32[]{:S(2)}) copy-start(bf16[24]{0:T(256)(128)(2,1)} %param.20) | copy-start | bytes 148
  3.8 2.7 %copy-start.11 = (bf16[24]{0:T(256)(128)(2,1)S(1)}, bf16[24]{0:T(256)(128)(2,1)}, u32[]{:S(2)}) copy-start(bf16[24]{0:T(256)(128)(2,1)} %param.26) | copy-start | bytes 148
  3.8 2.7 %copy-start.12 = (bf16[24]{0:T(256)(128)(2,1)S(1)}, bf16[24]{0:T(256)(128)(2,1)}, u32[]{:S(2)}) copy-start(bf16[24]{0:T(256)(128)(2,1)} %param.17) | copy-start | bytes 148
  3.8 2.7 %copy-start.13 = (bf16[24]{0:T(256)(128)(2,1)S(1)}, bf16[24]{0:T(256)(128)(2,1)}, u32[]{:S(2)}) copy-start(bf16[24]{0:T(256)(128)(2,1)} %param.18) | copy-start | bytes 148
  3.8 2.7 %copy-start.14 = (bf16[96]{0:T(256)(128)(2,1)S(1)}, bf16[96]{0:T(256)(128)(2,1)}, u32[]{:S(2)}) copy-start(bf16[96]{0:T(256)(128)(2,1)} %param.24) | copy-start | bytes 580
  5.0 2.2 %copy-start.2 = (bf16[96,768]{1,0:T(8,128)(2,1)S(1)}, bf16[96,768]{1,0:T(8,128)(2,1)}, u32[]{:S(2)}) copy-start(bf16[96,768]{1,0:T(8,128)(2,1)} %param.25) | copy-start | bytes 442372
  175.7 2.6 %copy-start.5 = (bf16[4,32,384]{2,1,0:T(8,128)(2,1)S(1)}, bf16[4,32,384]{2,1,0:T(8,128)(2,1)}, u32[]{:S(2)}) copy-start(bf16[4,32,384]{2,1,0:T(8,128)(2,1)} %get-tuple-element.25) | copy-start | bytes 294916
  175.7 2.6 %copy-start.4 = (bf16[4,32,384]{2,1,0:T(8,128)(2,1)S(1)}, bf16[4,32,384]{2,1,0:T(8,128)(2,1)}, u32[]{:S(2)}) copy-start(bf16[4,32,384]{2,1,0:T(8,128)(2,1)} %get-tuple-element.24) | copy-start | bytes 294916
  178.4 2.5 %copy-start.1 = (bf16[256,768]{1,0:T(8,128)(2,1)S(1)}, bf16[256,768]{1,0:T(8,128)(2,1)}, u32[]{:S(2)}) copy-start(bf16[256,768]{1,0:T(8,128)(2,1)} %get-tuple-element.70) | copy-start | bytes 1179652
  178.6 3.1 %copy-start = (bf16[256,768]{1,0:T(8,128)(2,1)S(1)}, bf16[256,768]{1,0:T(8,128)(2,1)}, u32[]{:S(2)}) copy-start(bf16[256,768]{1,0:T(8,128)(2,1)} %get-tuple-element.71) | copy-start | bytes 1179652

commit v2 on v1

--- a/solution.py
+++ b/solution.py
@@ -116,8 +116,8 @@
 
 
 class Ring:
-    def __init__(self, src, held, sends, recvs, own, order, f, s):
-        self.src, self.held, self.sends, self.recvs, self.own = src, held, sends, recvs, own
+    def __init__(self, src, held, sends, recvs, order, f, s):
+        self.src, self.held, self.sends, self.recvs = src, held, sends, recvs
         self.order, self.f, self.s = order, f, s
         self.y, self.h, self.z = f // 8, x_half(f), lax.rem(f, 4)
 
@@ -129,10 +129,11 @@
     def coordinate(self, axis, step):
         return lax.rem((self.y if axis == "y" else self.z) + step + 4, 4)
 
-    def one(self, axis, step, half=None):
-        i = self.coordinate(axis, step)
-        halves = slice(None) if half is None else half
-        return self.held.at[i, halves, self.z] if axis == "y" else self.held.at[self.y, halves, i]
+    def plane(self, t):
+        h = lax.rem(self.h + t // 4, 2)
+        if self.order[0] == "y":
+            return lax.rem(self.y + t, 4) * 8 + h * 4 + self.z, t // 4
+        return self.y * 8 + h * 4 + lax.rem(self.z + t, 4), t // 4
 
     def many(self, axis, step, half=None):
         i = self.coordinate(axis, step)
@@ -146,53 +147,39 @@
 
     def begin(self):
         mine = self.held.at[self.y, self.h, self.z]
-        other = lax.rem(self.s + 2, G)
-        send(
-            self.src.at[other], mine, self.sends.at[0], self.recvs.at[0], self.f + 4 - 8 * self.h, other
-        )
-        pltpu.make_async_copy(self.src.at[self.s], mine, self.own.at[0]).start()
-
-    def first(self):
-        mine = self.held.at[self.y, self.h, self.z]
-        take(mine, self.own.at[0])
-        take(mine, self.recvs.at[0])
-        axis = self.order[0]
-        self.push(self.one(axis, 0), 1, self.peer(axis, 1))
-        self.push(self.one(axis, 0), 2, self.peer(axis, -1))
-
-    def relay(self, part, base, axis):
-        take(part(axis, -1), self.recvs.at[base])
-        self.push(part(axis, -1, 0), base + 2, self.peer(axis, 1))
-        take(part(axis, 1), self.recvs.at[base + 1])
-        self.push(part(axis, 1, 1), base + 3, self.peer(axis, -1))
-
-    def first_relay(self):
-        self.relay(self.one, 1, self.order[0])
+
+        def one(t, k):
+            peer, away = self.plane(t)
+            group = lax.rem(self.s + 2 * away, G)
+            send(self.src.at[group], mine, self.sends.at[k], self.recvs.at[0], peer, group)
+
+        loop(4, lambda t: one(t + 4, 0))
+        loop(3, lambda t: one(t + 1, 7))
+        pltpu.make_async_copy(self.src.at[self.s], mine, self.recvs.at[0]).start()
 
     def last(self):
-        axis = self.order[0]
-        take(self.one(axis, 2, 0), self.recvs.at[3])
-        take(self.one(axis, 2, 1), self.recvs.at[4])
         axis = self.order[1]
-        self.push(self.many(axis, 0), 5, self.peer(axis, 1))
-        self.push(self.many(axis, 0), 6, self.peer(axis, -1))
+        take(self.many(axis, 0), self.recvs.at[0])
+        for k, (part, step) in enumerate(((0, 1), (1, -1), (1, 1), (0, -1))):
+            self.push(self.many(axis, 0, part), 1 + k, self.peer(axis, step))
 
     def last_relay(self):
-        self.relay(self.many, 5, self.order[1])
+        axis = self.order[1]
+        for k, step in enumerate((1, -1)):
+            part = self.many(axis, -step, k)
+            take(part, self.recvs.at[1 + k])
+            self.push(part, 5 + k, self.peer(axis, step))
 
     def arrive(self):
-        axis = self.order[1]
-        take(self.many(axis, 2, 0), self.recvs.at[7])
-        take(self.many(axis, 2, 1), self.recvs.at[8])
+        for k in (3, 4, 5, 6):
+            take(self.many(self.order[1], 0, 0), self.recvs.at[k])
 
     def drain(self):
-        one, many = self.order
-        take(self.held.at[self.y, self.h, self.z], self.sends.at[0])
-        for k in (1, 2):
-            take(self.one(one, 0), self.sends.at[k])
-            take(self.one(one, 0, 0), self.sends.at[k + 2])
-            take(self.many(many, 0), self.sends.at[k + 4])
-            take(self.many(many, 0, 0), self.sends.at[k + 6])
+        half = self.many(self.order[1], 0, 0)
+        take(half, self.sends.at[0])
+        take(self.held.at[0, 0, pl.ds(0, 3)], self.sends.at[7])
+        for k in range(1, 7):
+            take(half, self.sends.at[k])
 
 
 class Share:
@@ -202,8 +189,20 @@
         self.across = lax.rem(s + 2, G)
 
     def begin(self):
+        self.begin_across()
+        self.begin_twin()
+
+    def begin_all(self):
+        self.begin()
+        mine = self.block(self.s)
+        send(mine, mine, self.sends.at[2], self.recvs.at[2], self.f, 3 - self.s)
+
+    def begin_across(self):
         mine = self.block(self.s)
         send(mine, mine, self.sends.at[1], self.recvs.at[1], self.f, self.across)
+
+    def begin_twin(self):
+        mine = self.block(self.s)
         send(mine, mine, self.sends.at[0], self.recvs.at[0], self.f, self.twin)
 
     def relay(self):
@@ -215,6 +214,10 @@
         take(self.block(self.s), self.recvs.at[0])
         take(self.block(self.s), self.recvs.at[2])
 
+    def arrive_all(self):
+        self.arrive()
+        take(self.block(self.s), self.recvs.at[1])
+
     def drain(self):
         for k in range(3):
             take(self.block(self.s), self.sends.at[k])
@@ -222,24 +225,37 @@
 
 def greet_near(barrier, f, s):
     y, h, z = f // 8, x_half(f), lax.rem(f, 4)
-    greet(barrier, f + 4 - 8 * h, lax.rem(s + 2, G))
-    greet(barrier, f + 4 - 8 * h, s)
-    for step in (1, 3):
-        greet(barrier, lax.rem(y + step, 4) * 8 + lax.rem(f, 8), s)
-        greet(barrier, f - z + lax.rem(z + step, 4), s)
-    for step in (1, 2, 3):
-        greet(barrier, f, lax.rem(s + step, G))
-    pl.semaphore_wait(barrier, 9)
-
-
-def unpack_rings(held, first, wide):
-    c = held.shape[-1]
+    other = 1 - h
+
+    def line(t):
+        column, row = lax.rem(y + t, 4) * 8, lax.rem(z + t, 4)
+
+        @pl.when(t > 0)
+        def _():
+            greet(barrier, column + h * 4 + z, s)
+            greet(barrier, y * 8 + h * 4 + row, s)
+            greet(barrier, f, lax.rem(s + t, G))
+            for k in (0, 2):
+                greet(barrier, y * 8 + other * 4 + row, lax.rem(s + k, G))
+
+        for k in (0, 2):
+            greet(barrier, column + other * 4 + z, lax.rem(s + k, G))
+
+    loop(4, line)
+    pl.semaphore_wait(barrier, 23)
+
+
+def unpack_rings(pieces, wide):
+    c = wide.shape[-1] // 2
+
+    def block(y, h, z):
+        parts = [held[y, h, z, first : first + rows, :].astype(jnp.float32) for held, first, rows in pieces]
+        return parts[0] if len(parts) == 1 else jnp.concatenate(parts, axis=0)
 
     def pair(p):
         at = (p // 4, lax.rem(p // 2, 2))
         z = 2 * lax.rem(p, 2)
-        one = held[at[0], at[1], z, first : first + 48, :].astype(jnp.float32)
-        two = held[at[0], at[1], z + 1, first : first + 48, :].astype(jnp.float32)
+        one, two = block(*at, z), block(*at, z + 1)
         rows = pl.ds(pl.multiple_of(48 * p, 48), 48)
         wide[rows, :c] = jnp.concatenate([one[:ROWS], two[:ROWS]], axis=0).astype(wide.dtype)
         wide[rows, c:] = jnp.concatenate([one[ROWS:], two[ROWS:]], axis=0).astype(wide.dtype)
@@ -247,31 +263,28 @@
     loop(N // 2, pair)
 
 
-def spread_vectors(held, vec, f, s):
+def vector_masks(s):
     low, full = jnp.bfloat16, jnp.float32
     row = lax.broadcasted_iota(jnp.int32, (128, D), 0)
-    lane = lax.broadcasted_iota(jnp.int32, (128, D), 1)
-    inside = lax.rem(lane, ROWS)
-    plain = (row == inside).astype(full).astype(low)
-    shifted = (row == inside + ROWS * s).astype(full).astype(low)
-    owner = lax.broadcasted_iota(jnp.int32, (16, D), 1) // ROWS
-    number = lax.broadcasted_iota(jnp.int32, (16, D), 0)
-    vec[...] = jnp.zeros_like(vec)
-
-    def add(j):
-        block = held[j // 8, lax.rem(j // 4, 2), lax.rem(j, 4), 48:64, :128]
-        straight, moved = dot(block, plain), dot(block, shifted)
-        wanted = jnp.where(number < 7, j, jnp.where(j // 8 == s, lax.rem(j, 8), -1))
-        vec[...] += jnp.where(owner == wanted, jnp.where(number == 6, moved, straight), 0.0)
-
-    loop(N, add)
+    inside = lax.rem(lax.broadcasted_iota(jnp.int32, (128, D), 1), ROWS)
+    return (row == inside).astype(full).astype(low), (row == inside + ROWS * s).astype(full).astype(low)
+
+
+def spread_vectors(blocks, masks, s):
+    flat = blocks.reshape(N * 16, 128)
+    straight, moved = [dot(flat, mask).reshape(N, 16, D) for mask in masks]
+    owner = lax.broadcasted_iota(jnp.int32, (N, 16, D), 2) // ROWS
+    number = lax.broadcasted_iota(jnp.int32, (N, 16, D), 1)
+    j = lax.broadcasted_iota(jnp.int32, (N, 16, D), 0)
+    wanted = jnp.where(number < 7, j, jnp.where(j // 8 == s, j - 8 * s, -1))
+    return jnp.sum(jnp.where(owner == wanted, jnp.where(number == 6, moved, straight), 0.0), axis=0)
 
 
 class RingSum:
     def __init__(self, part, inbox, total, sends, recvs, order, f, s):
         self.part, self.inbox, self.total = part, inbox, total
         self.sends, self.recvs, self.f, self.s = sends, recvs, f, s
-        self.line = Ring(None, part, None, None, None, order, f, s)
+        self.line = Ring(None, part, None, None, order, f, s)
         self.order = order
 
     def push(self, block, inbox, k, peer):
@@ -283,47 +296,49 @@
             total = total + inbox[...].astype(jnp.float32)
         block[...] = total.astype(block.dtype)
 
-    def stage(self, section, axis, far, near, base):
-        line = self.line
-        self.push(section(axis, 2, 0), far.at[0], base, line.peer(axis, 1))
-        self.push(section(axis, 2, 1), far.at[1], base + 1, line.peer(axis, -1))
+    def steps(self):
+        line, axis = self.line, self.order[1]
+        far, plain, added, direct = self.inbox
+        sides = ((0, 1), (1, -1))
+        for k, step in sides:
+            self.push(line.many(axis, 2, k), far.at[k], k, line.peer(axis, step))
+        for k, step in sides:
+            self.push(line.many(axis, step, 1 - k), plain.at[k], 2 + k, line.peer(axis, step))
         yield
-        take(far.at[0], self.recvs.at[base])
-        self.add(section(axis, 1, 0), far.at[0])
-        self.push(section(axis, 1), near.at[0], base + 2, line.peer(axis, 1))
-        take(far.at[1], self.recvs.at[base + 1])
-        self.add(section(axis, -1, 1), far.at[1])
-        self.push(section(axis, -1), near.at[1], base + 3, line.peer(axis, -1))
+        for k, step in sides:
+            take(far.at[k], self.recvs.at[k])
+            self.add(line.many(axis, step, k), far.at[k])
+            self.push(line.many(axis, step, k), added.at[k], 4 + k, line.peer(axis, step))
         yield
-        take(near.at[0], self.recvs.at[base + 2])
-        take(near.at[1], self.recvs.at[base + 3])
-        self.add(section(axis, 0), near.at[0], near.at[1])
-
-    def steps(self):
-        line = self.line
-        far_many, near_many, far_one, near_one, beyond = self.inbox
-        yield from self.stage(line.many, self.order[1], far_many, near_many, 0)
-        yield from self.stage(line.one, self.order[0], far_one, near_one, 4)
-        self.push(
-            self.part.at[line.y, 1 - line.h, line.z], beyond, 8, (self.f + 4 - 8 * line.h, self.s)
-        )
+        for k, step in sides:
+            take(plain.at[1 - k], self.recvs.at[3 - k])
+            take(added.at[k], self.recvs.at[4 + k])
+            self.add(line.many(axis, 0, k), added.at[k], plain.at[1 - k])
+        first = line.y if self.order[0] == "y" else line.z
+        slot = 2 * first + line.h
+
+        def one(t):
+            peer, _ = line.plane(t + 1)
+            block = self.part.at[peer // 8, x_half(peer), lax.rem(peer, 4)]
+            send(block, direct.at[slot], self.sends.at[6], self.recvs.at[6], peer, self.s)
+
+        loop(7, one)
+        direct[slot] = self.part[line.y, line.h, line.z]
         yield
-        take(beyond, self.recvs.at[8])
-        mine = self.part[line.y, line.h, line.z].astype(jnp.float32)
-        self.total[self.s] = (mine + beyond[...].astype(jnp.float32)).astype(self.total.dtype)
+        take(direct.at[pl.ds(0, 7)], self.recvs.at[6])
+        self.total[self.s] = jnp.sum(direct[...].astype(jnp.float32), axis=0).astype(self.total.dtype)
 
     def drain(self):
-        far_many, near_many, far_one, near_one, beyond = self.inbox
-        for k, ref in enumerate((far_many, far_many, near_many, near_many, far_one, far_one, near_one, near_one)):
+        far, plain, added, direct = self.inbox
+        for k, ref in enumerate((far, far, plain, plain, added, added)):
             take(ref.at[0], self.sends.at[k])
-        take(beyond, self.sends.at[8])
+        take(direct.at[pl.ds(0, 7)], self.sends.at[6])
 
 
 def ring_inbox(order, rows):
-    many = (4, 2) if order[1] == "z" else (2, 4)
     half = (2, 2) if order[1] == "z" else (4,)
     block = (rows, 384)
-    return [(2,) + half + block, (2,) + many + block, (2,) + block, (2, 2) + block, block]
+    return [(2,) + half + block] * 3 + [(8,) + block]
 
 
 class SeqSum:
@@ -384,31 +399,32 @@
     return jnp.sum(values, axis=0, keepdims=True)
 
 
+GATHER_PLAN = (("yz", 32), ("zy", 32), ("yz", 80), ("zy", 64))
 RING_PLAN = (("yz", 48), ("zy", 48), ("yz", 16), ("yz", 32), ("zy", 32))
 
 
 def layer_kernel(*refs):
     (
-        src_a, src_b, src_c, src_x, src_dy,
+        src_a, src_b, src_c, src_d, src_x, src_dy,
         output, grad_input, fin_up, fin_down, fin_out, fin_a, fin_b,
         got_x, vec, normed, qkv, w_in, lse, got_ctx, w_out, w_up, w_down, got_dy,
-        held_a, held_b, held_c,
+        held_a, held_b, held_c, held_d,
         residual, normed_two, active, d_hidden, branch, d_ctx, d_proj, d_key, d_value, d_res, sums, grad_in,
         out_part, out_twins, out_crossed, two_part, two_twins, two_crossed, one_part, one_twins, one_crossed,
         part_up, part_down, part_out, part_a, part_b,
         *inboxes,
-        ring_ss, ring_rs, ring_own, seq_ss, seq_rs, seq_own, sum_ss, sum_rs, part_ss, part_rs,
+        ring_ss, ring_rs, seq_ss, seq_rs, seq_own, sum_ss, sum_rs, part_ss, part_rs,
     ) = refs
     low, full = jnp.bfloat16, jnp.float32
     f, s = place()
     greet_near(pltpu.get_barrier_semaphore(), f, s)
-    ring_a, ring_b, ring_c = [
-        Ring(src, held, ring_ss.at[k], ring_rs.at[k], ring_own.at[k], order, f, s)
-        for k, (src, held, order) in enumerate(
-            ((src_a, held_a, "yz"), (src_b, held_b, "zy"), (src_c, held_c, "yz"))
-        )
+    sources = (src_a, src_b, src_c, src_d)
+    helds = (held_a, held_b, held_c, held_d)
+    rings = [
+        Ring(sources[k], helds[k], ring_ss.at[k], ring_rs.at[k], GATHER_PLAN[k][0], f, s)
+        for k in range(4)
     ]
-    rings = (ring_a, ring_b, ring_c)
+    early, late = rings[:2], rings[2:]
     copies = [
         pltpu.make_async_copy(src, dst.at[s], seq_own.at[k])
         for k, (src, dst) in enumerate(((src_x, got_x), (src_dy, got_dy)))
@@ -423,20 +439,19 @@
     ]
     copies[0].wait()
     share_x.begin()
-    for ring in rings:
-        ring.first()
-    for ring in rings:
-        ring.first_relay()
-    for ring in rings:
+    masks = vector_masks(s)
+    for ring in early:
         ring.last()
+    for ring in early:
+        ring.last_relay()
     share_x.relay()
     copies[1].wait()
     share_dy.begin()
+    for ring in late:
+        ring.last()
     share_x.arrive()
-    for ring in rings:
-        ring.last_relay()
-    ring_a.arrive()
-    spread_vectors(held_a, vec, f, s)
+    rings[1].arrive()
+    vec[...] = spread_vectors(held_b[:, :, :, 16:, :128], masks, s)
     gain, shift = vec[0:1, :], vec[1:2, :]
 
     def norm_tile(t):
@@ -444,7 +459,8 @@
         normed[tile(t), :] = (unit * gain + shift).astype(normed.dtype)
 
     loop(G, norm_tile)
-    unpack_rings(held_a, 0, w_in)
+    rings[0].arrive()
+    unpack_rings(((held_a, 0, 32), (held_b, 0, 16)), w_in)
     bias = jnp.concatenate([vec[7:8, :PAD], jnp.zeros((1, PAD), jnp.float32), vec[8:9, :PAD]], axis=1)
 
     def project(t):
@@ -453,9 +469,12 @@
         qkv[tile(t), PAD:] = made[:, PAD:]
 
     loop(G, project)
-    share_dy.relay()
-    shares = []
-    for step, b in enumerate((3, 2, 1, 0)):
+    half = s // 2
+    shares = [
+        Share(lambda i, b=b: got_ctx.at[i, pl.ds(b * TOK, TOK)], seq_ss.at[2 + b], seq_rs.at[2 + b], f, s)
+        for b in range(G)
+    ]
+    for b in (1, 0, 3, 2):
         rows, span = slice(b * TOK, (b + 1) * TOK), (b + 1) * TOK
         for pair in range(2):
             at = pair * 128
@@ -470,23 +489,26 @@
                 part = dot(weights.astype(qkv.dtype), qkv[:span, 2 * PAD + at : 2 * PAD + at + 128]) / total
                 made = part if made is None else jnp.where(lanes_of(h, part.shape), part, made)
             got_ctx[s, rows, at : at + 128] = made.astype(got_ctx.dtype)
-        shares.append(
-            Share(
-                lambda i, b=b: got_ctx.at[i, pl.ds(b * TOK, TOK)], seq_ss.at[2 + step], seq_rs.at[2 + step], f, s
-            )
-        )
-        shares[-1].begin()
-        if step:
-            shares[step - 1].relay()
-    shares[-1].relay()
-    ring_b.arrive()
-    unpack_rings(held_b, 0, w_out)
-    unpack_rings(held_b, 48, w_up)
-    ring_c.arrive()
-    unpack_rings(held_c, 0, w_down)
+        shares[b].begin_twin()
+        if b > 1:
+            shares[b].begin_across()
+        else:
+            pl.when(half == 0)(shares[b].begin_across)
+
+    @pl.when(half == 1)
+    def _():
+        shares[1].begin_across()
+        shares[0].begin_across()
+
+    for ring in late:
+        ring.last_relay()
+    share_dy.relay()
+    for ring in late:
+        ring.arrive()
+    unpack_rings(((held_c, 0, 48),), w_out)
+    unpack_rings(((held_c, 48, 32), (held_d, 0, 16)), w_up)
+    unpack_rings(((held_d, 16, 48),), w_down)
     share_dy.arrive()
-    for share in shares:
-        share.arrive()
 
     sum_out = SeqSum(out_part, out_twins, out_crossed, part_ss.at[0], part_rs.at[0], f, s)
     sum_two = SeqSum(two_part, two_twins, two_crossed, part_ss.at[1], part_rs.at[1], f, s)
@@ -495,10 +517,19 @@
     gain_two, shift_two = vec[2:3, :], vec[3:4, :]
 
     def turn(i):
-        return jnp.where(i == 0, 3 - s, jnp.where(i == 1, lax.rem(s + 2, G), jnp.where(i == 2, sum_two.twin, s)))
+        return lax.rem(7 - 2 * half - i, G)
+
+    def context_at(t, action):
+        for b in range(G):
+            pl.when(t == b)(functools.partial(action, shares[b]))
+
+    def land(share):
+        share.relay()
+        share.arrive()
 
     def feed(i):
         t = turn(i)
+        context_at(t, land)
         rows = tile(t)
         value = got_x[t].astype(full) + vec[4:5, :]
         for g in range(G):
@@ -524,14 +555,13 @@
         out_part[t] = dot(active_low, w_down[...]).astype(low)
         sum_out.ready(t)
 
-        @pl.when(i > 1)
+        @pl.when(i > 0)
         def _():
             sum_two.relay(turn(i - 1))
-            sum_out.relay(turn(i - 1))
 
     loop(G, feed)
 
-    inbox = [inboxes[5 * k : 5 * k + 5] for k in range(5)]
+    inbox = [inboxes[4 * k : 4 * k + 4] for k in range(5)]
     totals = (fin_up, fin_down, fin_out, fin_a, fin_b)
     parts = (part_up, part_down, part_out, part_a, part_b)
     adders = [
@@ -543,11 +573,9 @@
 
     def life(k):
         yield from adders[k].steps()
-        finals[k].begin()
+        finals[k].begin_all()
         yield
-        finals[k].relay()
-        yield
-        finals[k].arrive()
+        finals[k].arrive_all()
 
     lives = [life(k) for k in range(5)]
 
@@ -556,20 +584,6 @@
             next(lives[k], None)
 
     cut_grad(normed_two, d_hidden, part_up, 0, 2)
-    advance(0)
-    flat_dy = [got_dy[t] for t in range(G)]
-    dy_all = jnp.concatenate(flat_dy, axis=0)
-
-    def chunk_down(c):
-        columns = pl.ds(pl.multiple_of(c * 384, 128), 384)
-        made = t_dot(active[:, columns], dy_all)
-        for i in range(16):
-            block = made[i * ROWS : (i + 1) * ROWS]
-            packed = jnp.concatenate([block[:, :384], block[:, 384:]], axis=0).astype(low)
-            part_down[2 * c + i // 8, (i // 4) % 2, i % 4] = packed
-
-    loop(2, chunk_down)
-    advance(1)
 
     mine = tile(s)
     own_res = residual[mine, :]
@@ -580,14 +594,28 @@
     branch[s] = d_own.astype(low)
     share_branch = Share(lambda i: branch.at[i], seq_ss.at[6], seq_rs.at[6], f, s)
     share_branch.begin()
+    advance(0)
     sums[4:5, :] += column_sum(d_own.astype(low).astype(full))
     sums[5:6, :] += column_sum(own_dy)
-    advance(0, 1)
-    share_branch.relay()
-    output[...] = (own_res + sum_out.total() + vec[5:6, :]).astype(low)
+    dy_all = jnp.concatenate([got_dy[t] for t in range(G)], axis=0)
+
+    def chunk_down(c):
+        columns = pl.ds(pl.multiple_of(c * 384, 128), 384)
+        made = t_dot(active[:, columns], dy_all)
+        for i in range(16):
+            block = made[i * ROWS : (i + 1) * ROWS]
+            packed = jnp.concatenate([block[:, :384], block[:, 384:]], axis=0).astype(low)
+            part_down[2 * c + i // 8, (i // 4) % 2, i % 4] = packed
+
+    loop(2, chunk_down)
+    advance(1)
     d_key[...] = jnp.zeros_like(d_key)
     d_value[...] = jnp.zeros_like(d_value)
+    share_branch.relay()
+    for t in range(G):
+        sum_out.relay(t)
     share_branch.arrive()
+    advance(0, 1)
 
     own_rows = pl.ds(pl.multiple_of(s * OWN, 64), OWN)
     pick = lax.broadcasted_iota(jnp.int32, (D, PAD), 0) == lax.broadcasted_iota(jnp.int32, (D, PAD), 1) + s * OWN
@@ -628,7 +656,8 @@
             if pair:
                 d_query = only(0, d_query)
             d_proj[rows, at : at + 128] = d_query.astype(low)
-            advance(0, 1, 2)
+        if b != 1:
+            advance(0, 1, 2) if b != 2 else advance(2)
         d_proj[rows, PAD : 2 * PAD] = d_key[rows, :].astype(low)
         d_proj[rows, 2 * PAD :] = d_value[rows, :].astype(low)
         d_one = dot_t(d_proj[rows, :], w_in[...])
@@ -669,11 +698,13 @@
 
     loop(2, cut_in)
     advance(3, 4)
+    output[...] = (own_res + sum_out.total() + vec[5:6, :]).astype(low)
+    advance(3, 4)
     advance(0, 1, 2)
+    advance(3, 4)
     unit, inverse = norm_parts(got_x[s].astype(full))
     grad_input[...] = (d_res[...] + norm_back(sum_one.total(), gain, unit, inverse)).astype(low)
-    for _ in range(8):
-        advance(3, 4)
+    advance(3, 4)
     for k in (0, 1, 2, 3, 4):
         for _ in lives[k]:
             pass
@@ -685,7 +716,7 @@
         adder.drain()
 
 
-def layer(src_a, src_b, src_c, inputs, cotangent):
+def layer(*sources):
     low, full = jnp.bfloat16, jnp.float32
     any_space, vmem = pl.BlockSpec(memory_space=pl.ANY), pl.BlockSpec(memory_space=pltpu.VMEM)
     outs = [jax.ShapeDtypeStruct((TOK, D), low)] * 2
@@ -694,7 +725,7 @@
     return pl.pallas_call(
         layer_kernel,
         out_shape=outs,
-        in_specs=[any_space] * 5,
+        in_specs=[any_space] * 6,
         out_specs=[vmem] * len(outs),
         scratch_shapes=[
             pltpu.VMEM((G, TOK, D), low),
@@ -709,7 +740,7 @@
             pltpu.VMEM((FFG, D), low),
             pltpu.VMEM((G, TOK, D), low),
         ]
-        + [pltpu.VMEM((4, 2, 4, rows, 384), low) for rows in (64, 96, 48)]
+        + [pltpu.VMEM((4, 2, 4, rows, 384), low) for _, rows in GATHER_PLAN]
         + [
             pltpu.VMEM((LEN, D), full),
             pltpu.VMEM((LEN, D), low),
@@ -727,8 +758,7 @@
         + seq_part * 3
         + [pltpu.VMEM((4, 2, 4, rows, 384), low) for _, rows in RING_PLAN]
         + [pltpu.VMEM(shape, low) for order, rows in RING_PLAN for shape in ring_inbox(order, rows)]
-        + [pltpu.SemaphoreType.DMA((3, 9))] * 2
-        + [pltpu.SemaphoreType.DMA((3, 1))]
+        + [pltpu.SemaphoreType.DMA((4, 9))] * 2
         + [pltpu.SemaphoreType.DMA((12, 3))] * 2
         + [pltpu.SemaphoreType.DMA((2,))]
         + [pltpu.SemaphoreType.DMA((5, 9))] * 2
@@ -736,7 +766,7 @@
         compiler_params=pltpu.CompilerParams(
             collective_id=0, has_side_effects=True, vmem_limit_bytes=62 * 2**20
         ),
-    )(src_a, src_b, src_c, inputs, cotangent)
+    )(*sources)
 
 
 def on_device(
@@ -768,10 +798,15 @@
     )
     compact = jnp.pad(vectors, ((0, 7), (0, 384 - ROWS)))
     compact = compact + jnp.pad(up_bias[None], ((6, 9), (0, 384 - 96)))
-    src_a = jnp.concatenate([send_in, jnp.broadcast_to(compact[None], (G, 16, 384))], axis=1)
-    src_b = jnp.concatenate([send_out, pack(units)], axis=1)
-    src_c = pack(down_weight.reshape(G, ROWS, D))
-    output, grad_input, all_up, all_down, all_out, all_a, all_b = layer(src_a, src_b, src_c, inputs, cotangent)
+    send_up = pack(units)
+    compact = jnp.broadcast_to(compact[None], (G, 16, 384))
+    src_a = send_in[:, :32]
+    src_b = jnp.concatenate([send_in[:, 32:], compact], axis=1)
+    src_c = jnp.concatenate([send_out, send_up[:, :32]], axis=1)
+    src_d = jnp.concatenate([send_up[:, 32:], pack(down_weight.reshape(G, ROWS, D))], axis=1)
+    output, grad_input, all_up, all_down, all_out, all_a, all_b = layer(
+        src_a, src_b, src_c, src_d, inputs, cotangent
+    )
     split_in = jnp.concatenate([all_a, all_b[:, :16]], axis=1)
     final_in = unpack(split_in.astype(full)).reshape(G, ROWS, 3, PAD)[..., :OWN].transpose(1, 2, 0, 3)
     final_up = unpack(all_up.astype(full)).reshape(G, ROWS, N, ROWS).transpose(1, 2, 0, 3).reshape(ROWS, G * FFG)

time: 183 us -> 141 us (0.77)
  Pallas kernels: 162 us -> 120 us
    pallas_call x1, Pallas kernels: 162 us -> 120 us  [layer(): pl.pallas_call(layer_kernel, out_shape=outs, in_specs=[any_space] * 6, ou...]
where the time goes in v2:
time: 141 us
  Pallas kernels  120 us (85%)
  local copies, waits for them, and re-layouts  14.9 us (11%)
  other arithmetic  4.32 us (3%)
    pallas_call x1, Pallas kernels, layer(): pl.pallas_call(layer_kernel, out_shape=outs, in_specs=[any_space] * 6, ou...  120 us
    reshape x2, local copies, waits for them, and re-layouts, on_device(): unpack(all_up.astype(full)).reshape(G, ROWS, N, ROWS).transpose(1, 2, 0, 3)  3.68 us
    reshape x2, local copies, waits for them, and re-layouts, on_device(): up_weight.reshape(ROWS, N, G, ROWS).transpose(2, 0, 1, 3)  3.35 us

profile of v2, /device:TPU:1, one launch (start us, length us, event | category | flops | bytes accessed | tf_op | source)
XLA Modules:
  0.0 140.7 jit_solution(12278645496034316009)
XLA Ops:
  0.6 2.1 %reshape.70 = bf16[24,32,4,24]{3,2,1,0:T(4,128)(2,1)S(1)} reshape(bf16[24,3072]{1,0:T(8,128)(2,1)} %param.23) | data formatting | bytes 294912 | tf_op jit(solution)/shard_map/reshape | solution.py:794
  2.8 0.0 copy-start.6
  2.8 0.0 copy-start.3
  2.8 0.1 copy.39
  2.9 1.2 reshape.71
  4.2 0.0 copy-start.2
  4.2 0.0 copy-done.6
  4.3 0.0 copy-start.7
  4.3 0.0 copy-start.8
  4.3 0.0 copy-start.9
  4.3 0.0 copy-start.10
  4.3 0.0 copy-start.11
  4.3 0.0 copy-start.12
  4.3 0.0 copy-start.13
  4.3 0.0 copy-start.14
  4.4 0.0 copy-start.15
  4.4 0.7 fusion.refs_2_
  5.1 0.0 copy-done.3
  5.1 0.2 reshape.68
  5.3 0.1 copy.44
  5.3 0.1 pad.12
  5.4 0.2 reshape.69
  5.6 0.7 pad_maximum_fusion.8.refs_0_
  6.3 0.0 copy-done.2
  6.3 0.7 pad_maximum_fusion.4.refs_3_
  7.0 0.0 copy-done.7
  7.1 0.0 copy-done.8
  7.1 0.0 copy-done.9
  7.1 0.1 stack.35
  7.2 0.7 pad_maximum_fusion.9.refs_1_
  7.9 120.4 %shard_map.262 = (bf16[256,768]{1,0:T(8,128)(2,1)}, bf16[256,768]{1,0:T(8,128)(2,1)}, bf16[4,48,384]{2,1,0:T(8,128)(2,1)}, bf16[4,48,384]{2,1,0:T(8,128)(2,1)}, ...) custom-call(bf16[4,32,384]{2,1,0:T(8,128)(2,1)} %pad_maximum_fusion.8.refs_0_, ...), custom_call_target="tpu_custom_call" | custom-call | tf_op jit(solution)/shard_map/pallas_call | solution.py:725
  128.3 0.8 slice_convert_fusion.1
  129.1 0.7 reshape.75
  129.9 1.0 fusion.3
  130.9 0.7 pad_maximum_fusion.2
  131.7 1.1 reshape.76
  132.8 1.2 copy.42
  134.1 2.5 %reshape.77 = f32[24,3072]{1,0:T(8,128)} reshape(f32[24,32,4,24]{3,2,1,0:T(4,128)S(1)} %copy.42) | data formatting | bytes 589824 | tf_op jit(solution)/shard_map/reshape | solution.py:812
  136.6 0.0 copy-done.4
  136.7 0.0 copy-start.1
  136.7 0.2 reshape.73
  136.9 0.1 slice_bitcast_fusion
  137.0 0.2 copy.40
  137.2 0.9 reshape.74
  138.1 0.5 slice_bitcast_fusion.1
  138.6 0.6 reshape.78
  139.2 0.7 copy.47
  140.0 0.7 copy.48
  (36 shorter events, 0.3 us)
Async XLA Ops:
  2.8 1.4 %copy-start.6 = (bf16[24,768]{1,0:T(8,128)(2,1)S(1)}, bf16[24,768]{1,0:T(8,128)(2,1)}, u32[]{:S(2)}) copy-start(bf16[24,768]{1,0:T(8,128)(2,1)} %param.19) | copy-start | bytes 110596
  2.8 2.3 %copy-start.3 = (bf16[24,2304]{1,0:T(8,128)(2,1)S(1)}, bf16[24,2304]{1,0:T(8,128)(2,1)}, u32[]{:S(2)}) copy-start(bf16[24,2304]{1,0:T(8,128)(2,1)} %param.16) | copy-start | bytes 331780
  4.2 2.1 %copy-start.2 = (bf16[96,768]{1,0:T(8,128)(2,1)S(1)}, bf16[96,768]{1,0:T(8,128)(2,1)}, u32[]{:S(2)}) copy-start(bf16[96,768]{1,0:T(8,128)(2,1)} %param.25) | copy-start | bytes 442372
  4.3 2.8 %copy-start.7 = (bf16[24]{0:T(256)(128)(2,1)S(1)}, bf16[24]{0:T(256)(128)(2,1)}, u32[]{:S(2)}) copy-start(bf16[24]{0:T(256)(128)(2,1)} %param.21) | copy-start | bytes 148
  4.3 2.8 %copy-start.8 = (bf16[24]{0:T(256)(128)(2,1)S(1)}, bf16[24]{0:T(256)(128)(2,1)}, u32[]{:S(2)}) copy-start(bf16[24]{0:T(256)(128)(2,1)} %param.22) | copy-start | bytes 148
  4.3 2.8 %copy-start.9 = (bf16[24]{0:T(256)(128)(2,1)S(1)}, bf16[24]{0:T(256)(128)(2,1)}, u32[]{:S(2)}) copy-start(bf16[24]{0:T(256)(128)(2,1)} %param.27) | copy-start | bytes 148
  4.3 2.8 %copy-start.10 = (bf16[24]{0:T(256)(128)(2,1)S(1)}, bf16[24]{0:T(256)(128)(2,1)}, u32[]{:S(2)}) copy-start(bf16[24]{0:T(256)(128)(2,1)} %param.28) | copy-start | bytes 148
  4.3 2.8 %copy-start.11 = (bf16[24]{0:T(256)(128)(2,1)S(1)}, bf16[24]{0:T(256)(128)(2,1)}, u32[]{:S(2)}) copy-start(bf16[24]{0:T(256)(128)(2,1)} %param.20) | copy-start | bytes 148
  4.3 2.8 %copy-start.12 = (bf16[24]{0:T(256)(128)(2,1)S(1)}, bf16[24]{0:T(256)(128)(2,1)}, u32[]{:S(2)}) copy-start(bf16[24]{0:T(256)(128)(2,1)} %param.26) | copy-start | bytes 148
  4.3 2.8 %copy-start.13 = (bf16[24]{0:T(256)(128)(2,1)S(1)}, bf16[24]{0:T(256)(128)(2,1)}, u32[]{:S(2)}) copy-start(bf16[24]{0:T(256)(128)(2,1)} %param.17) | copy-start | bytes 148
  4.3 2.8 %copy-start.14 = (bf16[24]{0:T(256)(128)(2,1)S(1)}, bf16[24]{0:T(256)(128)(2,1)}, u32[]{:S(2)}) copy-start(bf16[24]{0:T(256)(128)(2,1)} %param.18) | copy-start | bytes 148
  4.4 2.8 %copy-start.15 = (bf16[96]{0:T(256)(128)(2,1)S(1)}, bf16[96]{0:T(256)(128)(2,1)}, u32[]{:S(2)}) copy-start(bf16[96]{0:T(256)(128)(2,1)} %param.24) | copy-start | bytes 580
  134.1 2.6 %copy-start.5 = (bf16[4,32,384]{2,1,0:T(8,128)(2,1)S(1)}, bf16[4,32,384]{2,1,0:T(8,128)(2,1)}, u32[]{:S(2)}) copy-start(bf16[4,32,384]{2,1,0:T(8,128)(2,1)} %get-tuple-element.25) | copy-start | bytes 294916
  134.1 2.6 %copy-start.4 = (bf16[4,32,384]{2,1,0:T(8,128)(2,1)S(1)}, bf16[4,32,384]{2,1,0:T(8,128)(2,1)}, u32[]{:S(2)}) copy-start(bf16[4,32,384]{2,1,0:T(8,128)(2,1)} %get-tuple-element.24) | copy-start | bytes 294916
  136.7 2.5 %copy-start.1 = (bf16[256,768]{1,0:T(8,128)(2,1)S(1)}, bf16[256,768]{1,0:T(8,128)(2,1)}, u32[]{:S(2)}) copy-start(bf16[256,768]{1,0:T(8,128)(2,1)} %get-tuple-element.70) | copy-start | bytes 1179652
  136.9 3.1 %copy-start = (bf16[256,768]{1,0:T(8,128)(2,1)S(1)}, bf16[256,768]{1,0:T(8,128)(2,1)}, u32[]{:S(2)}) copy-start(bf16[256,768]{1,0:T(8,128)(2,1)} %get-tuple-element.71) | copy-start | bytes 1179652

commit v3 on v2

--- a/solution.py
+++ b/solution.py
@@ -235,14 +235,12 @@
             greet(barrier, column + h * 4 + z, s)
             greet(barrier, y * 8 + h * 4 + row, s)
             greet(barrier, f, lax.rem(s + t, G))
-            for k in (0, 2):
-                greet(barrier, y * 8 + other * 4 + row, lax.rem(s + k, G))
-
-        for k in (0, 2):
-            greet(barrier, column + other * 4 + z, lax.rem(s + k, G))
+            greet(barrier, y * 8 + other * 4 + row, lax.rem(s + 2, G))
+
+        greet(barrier, column + other * 4 + z, lax.rem(s + 2, G))
 
     loop(4, line)
-    pl.semaphore_wait(barrier, 23)
+    pl.semaphore_wait(barrier, 16)
 
 
 def unpack_rings(pieces, wide):
@@ -318,21 +316,30 @@
         slot = 2 * first + line.h
 
         def one(t):
-            peer, _ = line.plane(t + 1)
+            peer, away = line.plane(t + 1)
             block = self.part.at[peer // 8, x_half(peer), lax.rem(peer, 4)]
-            send(block, direct.at[slot], self.sends.at[6], self.recvs.at[6], peer, self.s)
+            group = lax.rem(self.s + 2 * away, G)
+            send(block, direct.at[slot], self.sends.at[6], self.recvs.at[6], peer, group)
 
         loop(7, one)
         direct[slot] = self.part[line.y, line.h, line.z]
         yield
         take(direct.at[pl.ds(0, 7)], self.recvs.at[6])
-        self.total[self.s] = jnp.sum(direct[...].astype(jnp.float32), axis=0).astype(self.total.dtype)
+        halves = direct[...].astype(jnp.float32).reshape(4, 2, *direct.shape[1:])
+        halves = jnp.sum(halves, axis=0).astype(self.total.dtype)
+        lower = line.h == 0
+        self.total[self.s, 0] = jnp.where(lower, halves[0], halves[1])
+        self.total[self.s, 1] = jnp.where(lower, halves[1], halves[0])
 
     def drain(self):
         far, plain, added, direct = self.inbox
         for k, ref in enumerate((far, far, plain, plain, added, added)):
             take(ref.at[0], self.sends.at[k])
         take(direct.at[pl.ds(0, 7)], self.sends.at[6])
+
+
+def joined(total, g):
+    return total[g, 0].astype(jnp.float32) + total[(g + 2) % G, 1].astype(jnp.float32)
 
 
 def ring_inbox(order, rows):
@@ -400,18 +407,19 @@
 
 
 GATHER_PLAN = (("yz", 32), ("zy", 32), ("yz", 80), ("zy", 64))
-RING_PLAN = (("yz", 48), ("zy", 48), ("yz", 16), ("yz", 32), ("zy", 32))
+RING_PLAN = (("yz", 48), ("zy", 48), ("zy", 16), ("yz", 32), ("zy", 16), ("yz", 16))
 
 
 def layer_kernel(*refs):
     (
         src_a, src_b, src_c, src_d, src_x, src_dy,
-        output, grad_input, fin_up, fin_down, fin_out, fin_a, fin_b,
+        output, grad_input, out_in, out_out, out_up, out_down, out_vec,
+        fin_up, fin_down, fin_out, fin_a, fin_b, fin_vec,
         got_x, vec, normed, qkv, w_in, lse, got_ctx, w_out, w_up, w_down, got_dy,
         held_a, held_b, held_c, held_d,
-        residual, normed_two, active, d_hidden, branch, d_ctx, d_proj, d_key, d_value, d_res, sums, grad_in,
+        residual, normed_two, active, d_hidden, branch, d_send, d_ctx, d_proj, d_key, d_value, d_res, sums,
         out_part, out_twins, out_crossed, two_part, two_twins, two_crossed, one_part, one_twins, one_crossed,
-        part_up, part_down, part_out, part_a, part_b,
+        part_up, part_down, part_out, part_a, part_b, part_vec,
         *inboxes,
         ring_ss, ring_rs, seq_ss, seq_rs, seq_own, sum_ss, sum_rs, part_ss, part_rs,
     ) = refs
@@ -561,14 +569,14 @@
 
     loop(G, feed)
 
-    inbox = [inboxes[4 * k : 4 * k + 4] for k in range(5)]
-    totals = (fin_up, fin_down, fin_out, fin_a, fin_b)
-    parts = (part_up, part_down, part_out, part_a, part_b)
+    inbox = [inboxes[4 * k : 4 * k + 4] for k in range(6)]
+    totals = (fin_up, fin_down, fin_out, fin_a, fin_b, fin_vec)
+    parts = (part_up, part_down, part_out, part_a, part_b, part_vec)
     adders = [
-        RingSum(parts[k], inbox[k], totals[k], sum_ss.at[k], sum_rs.at[k], RING_PLAN[k][0], f, s) for k in range(5)
+        RingSum(parts[k], inbox[k], totals[k], sum_ss.at[k], sum_rs.at[k], RING_PLAN[k][0], f, s) for k in range(6)
     ]
     finals = [
-        Share(lambda i, k=k: totals[k].at[i], seq_ss.at[7 + k], seq_rs.at[7 + k], f, s) for k in range(5)
+        Share(lambda i, k=k: totals[k].at[i], seq_ss.at[7 + k], seq_rs.at[7 + k], f, s) for k in range(6)
     ]
 
     def life(k):
@@ -577,7 +585,7 @@
         yield
         finals[k].arrive_all()
 
-    lives = [life(k) for k in range(5)]
+    lives = [life(k) for k in range(6)]
 
     def advance(*which):
         for k in which:
@@ -591,7 +599,14 @@
     own_dy = got_dy[s].astype(full)
     d_own = own_dy + norm_back(sum_two.total(), gain_two, unit, inverse)
     d_res[...] = d_own
-    branch[s] = d_own.astype(low)
+    own_branch = d_own.astype(low)
+    branch[s] = own_branch
+    for g in range(G):
+        made = dot_t(own_branch, w_out[g * OWN : (g + 1) * OWN, :])
+        d_send[g] = jnp.concatenate([made, jnp.zeros((TOK, PAD - OWN), full)], axis=1).astype(low)
+    for k, peer in enumerate((sum_two.across, sum_two.far_twin, sum_two.twin)):
+        send(d_send.at[peer], d_ctx.at[s], seq_ss.at[13, k], seq_rs.at[13, k], f, peer)
+    d_ctx[s] = d_send[s]
     share_branch = Share(lambda i: branch.at[i], seq_ss.at[6], seq_rs.at[6], f, s)
     share_branch.begin()
     advance(0)
@@ -611,33 +626,13 @@
     advance(1)
     d_key[...] = jnp.zeros_like(d_key)
     d_value[...] = jnp.zeros_like(d_value)
-    share_branch.relay()
-    for t in range(G):
-        sum_out.relay(t)
-    share_branch.arrive()
-    advance(0, 1)
-
-    own_rows = pl.ds(pl.multiple_of(s * OWN, 64), OWN)
-    pick = lax.broadcasted_iota(jnp.int32, (D, PAD), 0) == lax.broadcasted_iota(jnp.int32, (D, PAD), 1) + s * OWN
-    pick = jnp.logical_and(pick, lax.broadcasted_iota(jnp.int32, (D, PAD), 1) < OWN)
-    pick = pick.astype(full).astype(low)
-    picked = [dot(branch[t], pick).astype(low) for t in range(G)]
-    picked = jnp.concatenate(picked, axis=0)
-
-    def cut_out(g):
-        made = t_dot(got_ctx[g], picked)
-        for i in range(8):
-            one, two, three = [made[i * ROWS + 8 * r : i * ROWS + 8 * r + 8] for r in range(3)]
-            upper = jnp.concatenate([one, two[:, :128]], axis=1)
-            lower = jnp.concatenate([two[:, 128:], three], axis=1)
-            part_out[g, i // 4, i % 4] = jnp.concatenate([upper, lower], axis=0).astype(low)
-
-    loop(G, cut_out)
-    advance(2)
+    for k in range(3):
+        take(d_ctx.at[0], seq_rs.at[13, k])
+    advance(0)
+
     for b in (3, 2, 1, 0):
         rows, span = slice(b * TOK, (b + 1) * TOK), (b + 1) * TOK
-        made = dot_t(branch[b], w_out[own_rows, :])
-        d_block = jnp.concatenate([made, jnp.zeros((TOK, PAD - OWN), full)], axis=1).astype(low)
+        d_block = d_ctx[b]
         for pair in range(2):
             at = pair * 128
             d_query = None
@@ -656,20 +651,45 @@
             if pair:
                 d_query = only(0, d_query)
             d_proj[rows, at : at + 128] = d_query.astype(low)
-        if b != 1:
-            advance(0, 1, 2) if b != 2 else advance(2)
         d_proj[rows, PAD : 2 * PAD] = d_key[rows, :].astype(low)
         d_proj[rows, 2 * PAD :] = d_value[rows, :].astype(low)
-        d_one = dot_t(d_proj[rows, :], w_in[...])
-        one_part[b] = d_one.astype(low)
-        sum_one.ready(b)
-        unit, _ = norm_parts(got_x[b].astype(full))
+        if b == 3:
+            advance(1)
+        if b == 2:
+            advance(0)
+            for t in range(G):
+                sum_out.relay(t)
+
+    def cut_in(c):
+        columns = pl.ds(pl.multiple_of(c * 384, 128), 384)
+        made = t_dot(normed[:, columns], d_proj[...])
+        for i in range(16):
+            block = made[i * ROWS : (i + 1) * ROWS]
+            packed = jnp.concatenate([block[:, :384], block[:, 384:]], axis=0)
+            at = (2 * c + i // 8, (i // 4) % 2, i % 4)
+            part_a[at[0], at[1], at[2]] = packed[:32].astype(low)
+            part_b[at[0], at[1], at[2]] = packed[32:].astype(low)
+
+    loop(2, cut_in)
+    advance(3, 4)
+    advance(1)
+
+    def feed_back(i):
+        t = turn(i)
+        d_one = dot_t(d_proj[tile(t), :], w_in[...])
+        one_part[t] = d_one.astype(low)
+        sum_one.ready(t)
+        unit, _ = norm_parts(got_x[t].astype(full))
         sums[0:1, :] += column_sum(d_one * unit)
         sums[1:2, :] += column_sum(d_one)
-        if b < 3:
-            sum_one.relay(b + 1)
-    sum_one.relay(0)
-
+
+        @pl.when(i > 0)
+        def _():
+            sum_one.relay(turn(i - 1))
+
+    share_branch.relay()
+    loop(G, feed_back)
+    advance(0)
     sums[6:7, :PAD] = column_sum(d_proj[:, :PAD].astype(full))
     sums[7:8, :PAD] = column_sum(d_proj[:, 2 * PAD :].astype(full))
     lane = lax.broadcasted_iota(jnp.int32, (16, D), 1) // ROWS
@@ -681,35 +701,95 @@
     )
     compact = compact.astype(full).astype(low)
     pad_lanes = jnp.zeros((16, 256), low)
-
-    def cut_in(c):
-        columns = pl.ds(pl.multiple_of(c * 384, 128), 384)
-        made = t_dot(normed[:, columns], d_proj[...])
-        for i in range(16):
-            block = made[i * ROWS : (i + 1) * ROWS]
-            packed = jnp.concatenate([block[:, :384], block[:, 384:]], axis=0)
-            at = (2 * c + i // 8, (i // 4) % 2, i % 4)
-            part_a[at[0], at[1], at[2]] = packed[:32].astype(low)
-            part_b[at[0], at[1], at[2], :16, :] = packed[32:].astype(low)
-            owner = 16 * c + i
+    def cut_vec(g):
+        for i in range(8):
+            owner = 8 * g + i
             wanted = jnp.where(jnp.logical_or(number == 6, number == 7), owner - 8 * s, owner)
             few = dot(jnp.where(lane == wanted, plain, 0.0).astype(low), compact).astype(low)
-            part_b[at[0], at[1], at[2], 16:, :] = jnp.concatenate([few, pad_lanes], axis=1)
-
-    loop(2, cut_in)
+            part_vec[g, i // 4, i % 4] = jnp.concatenate([few, pad_lanes], axis=1)
+
+    loop(G, cut_vec)
+    advance(5)
+    pick_row = lax.broadcasted_iota(jnp.int32, (D, PAD), 0)
+    pick_lane = lax.broadcasted_iota(jnp.int32, (D, PAD), 1)
+    pick = jnp.where(pick_lane < OWN, pick_lane + s * OWN, -1) == pick_row
+    pick = pick.astype(full).astype(low)
+    share_branch.arrive()
+    picked = jnp.concatenate([dot(branch[t], pick).astype(low) for t in range(G)], axis=0)
+
+    def cut_out(g):
+        made = t_dot(got_ctx[g], picked)
+        for i in range(8):
+            one, two, three = [made[i * ROWS + 8 * r : i * ROWS + 8 * r + 8] for r in range(3)]
+            upper = jnp.concatenate([one, two[:, :128]], axis=1)
+            lower = jnp.concatenate([two[:, 128:], three], axis=1)
+            part_out[g, i // 4, i % 4] = jnp.concatenate([upper, lower], axis=0).astype(low)
+
+    loop(G, cut_out)
+    advance(2)
     advance(3, 4)
+    advance(1)
     output[...] = (own_res + sum_out.total() + vec[5:6, :]).astype(low)
+    place_row = lax.broadcasted_iota(jnp.int32, (PAD, D), 0)
+    place_lane = lax.broadcasted_iota(jnp.int32, (PAD, D), 1)
+    places = [
+        (jnp.where(place_row < OWN, place_row + g * OWN, -1) == place_lane).astype(full).astype(low)
+        for g in range(G)
+    ]
+    advance(5)
     advance(3, 4)
-    advance(0, 1, 2)
+    advance(0)
+    advance(2)
+    advance(1)
+    def place_up(g):
+        n = lax.broadcasted_iota(jnp.int32, (1, 1536), 1)
+        inside = lax.rem(n, 96) - ROWS * g
+        source = jnp.where(jnp.logical_and(inside >= 0, inside < ROWS), n // 96 * ROWS + inside, -1)
+        places = lax.broadcasted_iota(jnp.int32, (384, 1536), 0) == source
+        made = dot(joined(fin_up, g).astype(low), places.astype(full).astype(low))
+        out_up[:, :1536] += made[:ROWS]
+        out_up[:, 1536:] += made[ROWS:]
+
+    out_up[...] = jnp.zeros_like(out_up)
+    loop(G, place_up)
+    for g in range(G):
+        block = joined(fin_down, g)
+        out_down[g * ROWS : (g + 1) * ROWS, :384] = block[:ROWS]
+        out_down[g * ROWS : (g + 1) * ROWS, 384:] = block[ROWS:]
+    advance(5)
+    advance(2)
     advance(3, 4)
     unit, inverse = norm_parts(got_x[s].astype(full))
     grad_input[...] = (d_res[...] + norm_back(sum_one.total(), gain, unit, inverse)).astype(low)
+    advance(5, 2)
     advance(3, 4)
-    for k in (0, 1, 2, 3, 4):
+    total_in = jnp.zeros((3 * ROWS, D), full)
+    for g in range(G):
+        block = jnp.concatenate([joined(fin_a, g), joined(fin_b, g)], axis=0)
+        wide = jnp.concatenate([block[:ROWS], block[ROWS:]], axis=1)
+        tall = jnp.concatenate([wide[:, k * PAD : (k + 1) * PAD] for k in range(3)], axis=0)
+        total_in = total_in + dot(tall.astype(low), places[g])
+    for k in range(3):
+        out_in[:, k * D : (k + 1) * D] = total_in[k * ROWS : (k + 1) * ROWS]
+    advance(5, 2)
+    total_out = jnp.zeros((ROWS, D), full)
+    total_vec = jnp.zeros((16, 128), full)
+    for g in range(G):
+        both = joined(fin_out, g)
+        upper, lower = both[:8], both[8:]
+        middle = jnp.concatenate([upper[:, PAD:], lower[:, :128]], axis=1)
+        block = jnp.concatenate([upper[:, :PAD], middle, lower[:, 128:]], axis=0)
+        total_out = total_out + dot(block.astype(low), places[g])
+        total_vec = total_vec + joined(fin_vec, g)[:, :128]
+    out_out[...] = total_out
+    out_vec[...] = total_vec
+    for k in range(6):
         for _ in lives[k]:
             pass
     for share in [share_x, share_dy, share_branch] + shares + finals:
         share.drain()
+    for k in range(3):
+        take(d_send.at[0], seq_ss.at[13, k])
     for ring in rings:
         ring.drain()
     for adder in adders + [sum_out, sum_two, sum_one]:
@@ -720,14 +800,18 @@
     low, full = jnp.bfloat16, jnp.float32
     any_space, vmem = pl.BlockSpec(memory_space=pl.ANY), pl.BlockSpec(memory_space=pltpu.VMEM)
     outs = [jax.ShapeDtypeStruct((TOK, D), low)] * 2
-    outs += [jax.ShapeDtypeStruct((G, rows, 384), low) for _, rows in RING_PLAN]
+    outs += [
+        jax.ShapeDtypeStruct(shape, full)
+        for shape in ((ROWS, 3 * D), (ROWS, D), (ROWS, G * FFG), (G * ROWS, D), (16, 128))
+    ]
     seq_part = [pltpu.VMEM((G, TOK, D), low), pltpu.VMEM((2, TOK, D), low), pltpu.VMEM((TOK, D), low)]
     return pl.pallas_call(
         layer_kernel,
         out_shape=outs,
         in_specs=[any_space] * 6,
         out_specs=[vmem] * len(outs),
-        scratch_shapes=[
+        scratch_shapes=[pltpu.VMEM((G, 2, rows, 384), low) for _, rows in RING_PLAN]
+        + [
             pltpu.VMEM((G, TOK, D), low),
             pltpu.VMEM((16, D), full),
             pltpu.VMEM((LEN, D), low),
@@ -747,21 +831,21 @@
             pltpu.VMEM((LEN, FFG), low),
             pltpu.VMEM((LEN, FFG), low),
             pltpu.VMEM((G, TOK, D), low),
-            pltpu.VMEM((16, PAD), low),
+            pltpu.VMEM((G, TOK, PAD), low),
+            pltpu.VMEM((G, TOK, PAD), low),
             pltpu.VMEM((LEN, 3 * PAD), low),
             pltpu.VMEM((LEN, PAD), full),
             pltpu.VMEM((LEN, PAD), full),
             pltpu.VMEM((TOK, D), full),
-            pltpu.VMEM((16, D), full),
             pltpu.VMEM((16, D), full),
         ]
         + seq_part * 3
         + [pltpu.VMEM((4, 2, 4, rows, 384), low) for _, rows in RING_PLAN]
         + [pltpu.VMEM(shape, low) for order, rows in RING_PLAN for shape in ring_inbox(order, rows)]
         + [pltpu.SemaphoreType.DMA((4, 9))] * 2
-        + [pltpu.SemaphoreType.DMA((12, 3))] * 2
+        + [pltpu.SemaphoreType.DMA((14, 3))] * 2
         + [pltpu.SemaphoreType.DMA((2,))]
-        + [pltpu.SemaphoreType.DMA((5, 9))] * 2
+        + [pltpu.SemaphoreType.DMA((6, 9))] * 2
         + [pltpu.SemaphoreType.DMA((3, 3))] * 2,
         compiler_params=pltpu.CompilerParams(
             collective_id=0, has_side_effects=True, vmem_limit_bytes=62 * 2**20
@@ -804,22 +888,14 @@
     src_b = jnp.concatenate([send_in[:, 32:], compact], axis=1)
     src_c = jnp.concatenate([send_out, send_up[:, :32]], axis=1)
     src_d = jnp.concatenate([send_up[:, 32:], pack(down_weight.reshape(G, ROWS, D))], axis=1)
-    output, grad_input, all_up, all_down, all_out, all_a, all_b = layer(
+    output, grad_input, final_in, final_out, final_up, final_down, final_vec = layer(
         src_a, src_b, src_c, src_d, inputs, cotangent
     )
-    split_in = jnp.concatenate([all_a, all_b[:, :16]], axis=1)
-    final_in = unpack(split_in.astype(full)).reshape(G, ROWS, 3, PAD)[..., :OWN].transpose(1, 2, 0, 3)
-    final_up = unpack(all_up.astype(full)).reshape(G, ROWS, N, ROWS).transpose(1, 2, 0, 3).reshape(ROWS, G * FFG)
-    upper, lower = all_out[:, :8].astype(full), all_out[:, 8:].astype(full)
-    second = jnp.concatenate([upper[..., PAD:], lower[..., :128]], axis=-1)
-    out_blocks = jnp.concatenate([upper[..., :PAD], second, lower[..., 128:]], axis=1)
-    final_out = out_blocks[..., :OWN].transpose(1, 0, 2).reshape(ROWS, D)
-    final_down = unpack(all_down.astype(full)).reshape(96, D)
-    final_vec = jnp.sum(all_b[:, 16:, :ROWS].astype(full), axis=0)
+    final_vec = final_vec[:, :ROWS]
     return (
         output,
         grad_input,
-        final_in.reshape(ROWS, 3 * D),
+        final_in,
         final_vec[6],
         final_vec[7],
         final_out,

time: 141 us -> 134 us (0.950)
  Pallas kernels: 120 us -> 116 us
  other arithmetic: 4.32 us -> 2.13 us
    unnamed x34 -> x44, local copies, waits for them, and re-layouts: 1.58 us -> 11 us
    reshape x5 -> x0, local copies, waits for them, and re-layouts: 5.45 us -> none  [the longest x2 3.68 us: on_device(): unpack(all_up.astype(full)).reshape(G, ROWS, N, ROWS).transpose(1, 2, 0, 3)]
    pallas_call x1, Pallas kernels: 120 us -> 116 us  [layer(): pl.pallas_call(layer_kernel, out_shape=outs, in_specs=[any_space] * 6, ou...]
    transpose x4 -> x0, local copies, waits for them, and re-layouts: 1.55 us -> none  [the longest x1 1.25 us: on_device(): unpack(all_up.astype(full)).reshape(G, ROWS, N, ROWS).transpose(1, 2, 0, 3)]
    concatenate x4 -> x0, other arithmetic: 1.43 us -> none  [the longest x3 0.78 us: unpack(): jnp.concatenate([blocks[..., :ROWS, :], blocks[..., ROWS:, :]], axis=-1)]
where the time goes in v3:
time: 134 us
  Pallas kernels  116 us (87%)
  local copies, waits for them, and re-layouts  15.3 us (11%)
  other arithmetic  2.13 us (2%)
    pallas_call x1, Pallas kernels, layer(): pl.pallas_call(layer_kernel, out_shape=outs, in_specs=[any_space] * 6, ou...  116 us
    unnamed x44, local copies, waits for them, and re-layouts  11 us

profile of v3, /device:TPU:1, one launch (start us, length us, event | category | flops | bytes accessed | tf_op | source)
XLA Modules:
  0.0 134.0 jit_solution(14933053181596375925)
XLA Ops:
  0.6 0.0 copy-start.17
  0.7 0.0 copy-start.13
  0.7 0.0 copy-start.14
  0.7 0.0 copy-start.15
  0.7 0.0 copy-start.16
  0.7 0.0 copy-start.10
  0.7 0.0 copy-start.11
  0.7 0.0 copy-start.12
  0.7 0.6 copy-done.17
  1.3 0.0 copy-done.13
  1.3 0.0 copy-done.14
  1.3 0.0 copy-done.15
  1.4 0.0 copy-done.16
  1.4 0.0 copy-done.10
  1.4 0.0 copy-done.11
  1.4 0.0 copy-done.12
  1.4 0.1 stack.35
  1.5 0.6 copy-done.18
  2.1 0.7 copy-done.8
  2.9 0.0 copy-start.6
  2.9 0.9 copy-done.6
  3.8 0.2 reshape.50
  3.9 0.1 copy.35
  4.0 0.1 pad.12
  4.1 0.2 reshape.51
  4.3 0.0 copy-start.5
  4.3 0.7 pad_maximum_fusion.2
  5.0 0.3 copy-done.5
  5.3 0.9 copy-done.4
  6.2 1.2 reshape.52
  7.4 0.1 copy.33
  7.6 1.2 reshape.53
  8.8 0.7 pad_maximum_fusion.1.refs_3_
  9.5 0.7 fusion.refs_2_
  10.2 115.7 %shard_map.262 = (bf16[256,768]{1,0:T(8,128)(2,1)}, bf16[256,768]{1,0:T(8,128)(2,1)}, f32[24,2304]{1,0:T(8,128)}, f32[24,768]{1,0:T(8,128)}, f32[24,3072]{1,0:T(...) custom-call(bf16[4,32,384]{2,1,0:T(8,128)(2,1)} %get-tuple-element.45.refs_0_, ...), custom_call_target="tpu_custom_call" | custom-call | tf_op jit(solution)/shard_map/pallas_call | solution.py:808
  125.9 0.0 copy-start.9
  125.9 0.7 copy-done.9
  126.6 0.5 slice_bitcast_fusion
  127.2 0.6 reshape.55
  127.8 1.8 %copy.42 = bf16[256,768]{1,0:T(8,128)(2,1)} copy(bf16[256,768]{1,0:T(8,128)(2,1)} %get-tuple-element.62) | data formatting | bytes 786432
  129.6 0.7 copy.43
  130.3 0.3 copy-done.3
  130.7 0.7 copy.44
  131.3 0.2 copy-done.7
  131.6 0.6 copy.45
  132.2 0.7 copy.46
  132.9 0.4 copy-done.1
  133.3 0.7 copy.47
  (22 shorter events, 0.1 us)
Async XLA Ops:
  0.6 0.7 copy-start.17
  0.7 0.7 copy-start.13
  0.7 0.7 copy-start.14
  0.7 0.7 copy-start.15
  0.7 0.7 copy-start.16
  0.7 0.7 copy-start.10
  0.7 0.7 copy-start.11
  0.7 0.7 copy-start.12
  1.4 0.7 copy-start.18
  2.1 0.8 copy-start.8
  2.9 0.9 copy-start.6
  4.3 1.0 copy-start.5
  5.3 0.9 copy-start.4
  125.9 0.7 copy-start.9
  127.8 1.8 %copy-start = (bf16[256,768]{1,0:T(8,128)(2,1)S(1)}, bf16[256,768]{1,0:T(8,128)(2,1)}, u32[]{:S(2)}) copy-start(bf16[256,768]{1,0:T(8,128)(2,1)} %get-tuple-element.63) | copy-start | bytes 1179652
  129.6 1.1 copy-start.3
  130.7 0.9 copy-start.7
  130.7 1.5 %copy-start.2 = (f32[24,3072]{1,0:T(8,128)S(1)}, f32[24,3072]{1,0:T(8,128)}, u32[]{:S(2)}) copy-start(f32[24,3072]{1,0:T(8,128)} %get-tuple-element.71) | copy-start | bytes 884740
  132.2 1.1 copy-start.1

commit v4 on v3

--- a/solution.py
+++ b/solution.py
@@ -413,7 +413,7 @@
 def layer_kernel(*refs):
     (
         src_a, src_b, src_c, src_d, src_x, src_dy,
-        output, grad_input, out_in, out_out, out_up, out_down, out_vec,
+        out_rows, out_wide, out_down, out_vec,
         fin_up, fin_down, fin_out, fin_a, fin_b, fin_vec,
         got_x, vec, normed, qkv, w_in, lse, got_ctx, w_out, w_up, w_down, got_dy,
         held_a, held_b, held_c, held_d,
@@ -729,7 +729,7 @@
     advance(2)
     advance(3, 4)
     advance(1)
-    output[...] = (own_res + sum_out.total() + vec[5:6, :]).astype(low)
+    out_rows[:TOK, :] = (own_res + sum_out.total() + vec[5:6, :]).astype(low)
     place_row = lax.broadcasted_iota(jnp.int32, (PAD, D), 0)
     place_lane = lax.broadcasted_iota(jnp.int32, (PAD, D), 1)
     places = [
@@ -747,10 +747,10 @@
         source = jnp.where(jnp.logical_and(inside >= 0, inside < ROWS), n // 96 * ROWS + inside, -1)
         places = lax.broadcasted_iota(jnp.int32, (384, 1536), 0) == source
         made = dot(joined(fin_up, g).astype(low), places.astype(full).astype(low))
-        out_up[:, :1536] += made[:ROWS]
-        out_up[:, 1536:] += made[ROWS:]
-
-    out_up[...] = jnp.zeros_like(out_up)
+        out_wide[:, 4 * D : 6 * D] += made[:ROWS]
+        out_wide[:, 6 * D :] += made[ROWS:]
+
+    out_wide[:, 4 * D :] = jnp.zeros((ROWS, 4 * D), full)
     loop(G, place_up)
     for g in range(G):
         block = joined(fin_down, g)
@@ -760,7 +760,7 @@
     advance(2)
     advance(3, 4)
     unit, inverse = norm_parts(got_x[s].astype(full))
-    grad_input[...] = (d_res[...] + norm_back(sum_one.total(), gain, unit, inverse)).astype(low)
+    out_rows[TOK:, :] = (d_res[...] + norm_back(sum_one.total(), gain, unit, inverse)).astype(low)
     advance(5, 2)
     advance(3, 4)
     total_in = jnp.zeros((3 * ROWS, D), full)
@@ -770,7 +770,7 @@
         tall = jnp.concatenate([wide[:, k * PAD : (k + 1) * PAD] for k in range(3)], axis=0)
         total_in = total_in + dot(tall.astype(low), places[g])
     for k in range(3):
-        out_in[:, k * D : (k + 1) * D] = total_in[k * ROWS : (k + 1) * ROWS]
+        out_wide[:, k * D : (k + 1) * D] = total_in[k * ROWS : (k + 1) * ROWS]
     advance(5, 2)
     total_out = jnp.zeros((ROWS, D), full)
     total_vec = jnp.zeros((16, 128), full)
@@ -781,7 +781,7 @@
         block = jnp.concatenate([upper[:, :PAD], middle, lower[:, 128:]], axis=0)
         total_out = total_out + dot(block.astype(low), places[g])
         total_vec = total_vec + joined(fin_vec, g)[:, :128]
-    out_out[...] = total_out
+    out_wide[:, 3 * D : 4 * D] = total_out
     out_vec[...] = total_vec
     for k in range(6):
         for _ in lives[k]:
@@ -799,10 +799,10 @@
 def layer(*sources):
     low, full = jnp.bfloat16, jnp.float32
     any_space, vmem = pl.BlockSpec(memory_space=pl.ANY), pl.BlockSpec(memory_space=pltpu.VMEM)
-    outs = [jax.ShapeDtypeStruct((TOK, D), low)] * 2
+    outs = [jax.ShapeDtypeStruct((2 * TOK, D), low)]
     outs += [
         jax.ShapeDtypeStruct(shape, full)
-        for shape in ((ROWS, 3 * D), (ROWS, D), (ROWS, G * FFG), (G * ROWS, D), (16, 128))
+        for shape in ((ROWS, 8 * D), (G * ROWS, D), (16, 128))
     ]
     seq_part = [pltpu.VMEM((G, TOK, D), low), pltpu.VMEM((2, TOK, D), low), pltpu.VMEM((TOK, D), low)]
     return pl.pallas_call(
@@ -888,21 +888,19 @@
     src_b = jnp.concatenate([send_in[:, 32:], compact], axis=1)
     src_c = jnp.concatenate([send_out, send_up[:, :32]], axis=1)
     src_d = jnp.concatenate([send_up[:, 32:], pack(down_weight.reshape(G, ROWS, D))], axis=1)
-    output, grad_input, final_in, final_out, final_up, final_down, final_vec = layer(
-        src_a, src_b, src_c, src_d, inputs, cotangent
-    )
+    final_rows, final_wide, final_down, final_vec = layer(src_a, src_b, src_c, src_d, inputs, cotangent)
     final_vec = final_vec[:, :ROWS]
     return (
-        output,
-        grad_input,
-        final_in,
+        final_rows[:TOK],
+        final_rows[TOK:],
+        final_wide[:, : 3 * D],
         final_vec[6],
         final_vec[7],
-        final_out,
+        final_wide[:, 3 * D : 4 * D],
         final_vec[4],
         final_vec[0],
         final_vec[1],
-        final_up,
+        final_wide[:, 4 * D :],
         final_vec[8:12].reshape(96),
         final_down,
         final_vec[5],

time: 134 us -> 133 us (level)
  local copies, waits for them, and re-layouts: 15.3 us -> 13.7 us
    unnamed x44 -> x33, local copies, waits for them, and re-layouts: 11 us -> 5.1 us
    slice x0 -> x4, local copies, waits for them, and re-layouts: none -> 4.17 us  [the longest x1 2.1 us: on_device(): final_rows[TOK:]]
where the time goes in v4:
time: 133 us; the launch traced here: 132 us
  Pallas kernels  116 us (87%)
  local copies, waits for them, and re-layouts  13.7 us (10%)
  other arithmetic  2.13 us (2%)
    pallas_call x1, Pallas kernels, layer(): pl.pallas_call(layer_kernel, out_shape=outs, in_specs=[any_space] * 6, ou...  116 us
    unnamed x33, local copies, waits for them, and re-layouts  5.1 us

profile of v4, /device:TPU:1, one launch (start us, length us, event | category | flops | bytes accessed | tf_op | source)
XLA Modules:
  0.0 132.3 jit_solution(17082429019207664798)
XLA Ops:
  0.6 0.0 copy-start.14
  0.7 0.0 copy-start.10
  0.7 0.0 copy-start.11
  0.7 0.0 copy-start.12
  0.7 0.0 copy-start.13
  0.7 0.0 copy-start.7
  0.7 0.0 copy-start.8
  0.7 0.0 copy-start.9
  0.7 0.6 copy-done.14
  1.3 0.0 copy-done.10
  1.3 0.0 copy-done.11
  1.3 0.0 copy-done.12
  1.4 0.0 copy-done.13
  1.4 0.0 copy-done.7
  1.4 0.0 copy-done.8
  1.4 0.0 copy-done.9
  1.4 0.0 copy-start.15
  1.4 0.1 stack.35
  1.5 0.6 copy-done.15
  2.1 0.7 copy-done.5
  2.9 0.0 copy-start.4
  2.9 0.9 copy-done.4
  3.8 0.2 reshape.50
  3.9 0.1 copy.35
  4.0 0.1 pad.12
  4.1 0.2 reshape.51
  4.3 0.0 copy-start.3
  4.3 0.7 pad_maximum_fusion.2
  5.0 0.3 copy-done.3
  5.3 0.9 copy-done.2
  6.2 1.2 reshape.52
  7.4 0.1 copy.33
  7.6 1.2 reshape.53
  8.8 0.7 pad_maximum_fusion.1.refs_3_
  9.5 0.7 fusion.refs_2_
  10.2 115.7 %shard_map.262 = (bf16[512,768]{1,0:T(8,128)(2,1)}, f32[24,6144]{1,0:T(8,128)}, f32[96,768]{1,0:T(8,128)}, f32[16,128]{1,0:T(8,128)}) custom-call(bf16[4,32,384]{2,1,0:T(8,128)(2,1)} %get-tuple-element.41.refs_0_, bf16[4,32,384]{2,1,0:T(8,128)(2,1)} %get-tuple-element.42.refs_1_, bf16[4,80,384]{2,1,0:T(8,128)(2,1)} %fusion.refs_2_, ...), custom_call_target="tpu_custom_call" | custom-call | tf_op jit(solution)/shard_map/pallas_call | solution.py:808
  125.9 0.0 copy-start.6
  125.9 0.0 copy-start
  125.9 2.1 %fusion.1 = (bf16[256,768]{1,0:T(8,128)(2,1)}, bf16[256,768]{1,0:T(8,128)(2,1)}) fusion(bf16[512,768]{1,0:T(8,128)(2,1)} %get-tuple-element.19), kind=kLoop, calls=%fused_computation.16 | loop fusion | bytes 1572864 | tf_op jit(solution)/shard_map/slice | solution.py:895
  128.0 0.0 copy-done.6
  128.0 0.5 slice_bitcast_fusion
  128.6 0.6 reshape.55
  129.2 0.0 copy-done
  129.2 0.6 slice.107
  129.8 0.7 slice.104
  130.5 0.7 slice.111
  131.3 0.3 copy-done.1
  131.6 0.7 copy.37
  (15 shorter events, 0.1 us)
Async XLA Ops:
  0.6 0.7 copy-start.14
  0.7 0.7 copy-start.10
  0.7 0.7 copy-start.11
  0.7 0.7 copy-start.12
  0.7 0.7 copy-start.13
  0.7 0.7 copy-start.7
  0.7 0.7 copy-start.8
  0.7 0.7 copy-start.9
  1.4 0.7 copy-start.15
  2.1 0.8 copy-start.5
  2.9 0.9 copy-start.4
  4.3 1.0 copy-start.3
  5.3 0.9 copy-start.2
  125.9 2.1 %copy-start.6 = (f32[16,128]{1,0:T(8,128)S(1)}, f32[16,128]{1,0:T(8,128)}, u32[]{:S(2)}) copy-start(f32[16,128]{1,0:T(8,128)} %get-tuple-element.21) | copy-start | bytes 24580
  125.9 3.3 %copy-start = (f32[24,6144]{1,0:T(8,128)S(1)}, f32[24,6144]{1,0:T(8,128)}, u32[]{:S(2)}) copy-start(f32[24,6144]{1,0:T(8,128)} %get-tuple-element.20) | copy-start | bytes 1769476
  130.5 1.1 copy-start.1
